TPU v7x, 256 devices: a whole 4x4x8 slice. The times are simulated.
256 devices in a mesh: sub: 128 (over z, y, x), col: 2 (over core).
Axes of the slice: x: 4, y: 4, z: 8, core: 2. Of those that a mesh axis runs over, the one named last changes fastest.
Arguments:
- prolong: bfloat16 [524288, 256], P('sub', 'col'), may hold values from -2.390625 to 2.390625
- tiles: bfloat16 [128, 5, 96, 128, 128], P('sub', None, 'col'), may hold values from -0.046875 to 0.046875
- tile_rows: int32 [128, 5, 96], P('sub', None, 'col'), may hold values from 0 to 31
- tile_cols: int32 [128, 5, 96], P('sub', None, 'col'), may hold values from 0 to 31
- counts: int32 [128, 5], P('sub'), may hold values from 32 to 96
Outputs:
- coarse_upper: float32 [128, 5, 256, 256], P('sub', None, 'col')
- coarse_lower: float32 [128, 4, 256, 256], P('sub', None, None, 'col')
Inputs may be any that keep to these rules, and one draw needn't show every extreme that they name: Slots at and beyond counts are ignored; counts reach 96 for some subdomain and offset.
All inputs are finite; a program needn't handle non-finite values.
Results may differ from a plain program's by a relative error of at most 0.0029.
Values may be sent and summed in bfloat16 or wider, within the bound.
No kernel may reach another device: no remote copies, remote signals or barrier semaphores. Data moves between devices by JAX's collectives and lax.ppermute only.
A program may use at most 128 MiB of HBM per device.

v0:
```python
import jax
import jax.numpy as jnp
from jax import lax
from jax.sharding import PartitionSpec as P


def passed_along(block, axis, distance):
    devices = range(lax.axis_size(axis))
    route = [(i - distance, i) for i in devices if i - distance in devices]
    return lax.ppermute(block, axis, route)


def form_block(own_tiles, far_full, a_tiles, rows_idx, cols_idx, live):
    width = far_full.shape[1]
    far_tiles = far_full.reshape(-1, a_tiles.shape[1], width)
    applied = jnp.einsum(
        "pkl,plc->pkc", a_tiles, far_tiles[cols_idx], preferred_element_type=jnp.float32
    )
    applied = (applied * live[:, None, None]).astype(jnp.bfloat16)
    return jnp.einsum(
        "pkr,pkc->rc", own_tiles[rows_idx], applied, preferred_element_type=jnp.float32
    )


def on_device(prolong, tiles, tile_rows, tile_cols, counts):
    slots = tiles.shape[2]
    edge = tiles.shape[3]
    offsets = tiles.shape[1] - 1
    first_slot = lax.axis_index("col") * slots
    own_full = lax.all_gather(prolong, "col", axis=1, tiled=True)
    width = own_full.shape[1]
    own_tiles = own_full.reshape(-1, edge, width)
    panels = [own_full]
    for offset in range(1, offsets + 1):
        got = passed_along(own_full, "sub", -offset)
        panels.append(got)
    slot_ids = first_slot + jnp.arange(slots, dtype=jnp.int32)
    blocks = []
    for offset in range(offsets + 1):
        live = (slot_ids < counts[0, offset]).astype(jnp.float32)
        blocks.append(
            form_block(
                own_tiles,
                panels[offset],
                tiles[0, offset],
                tile_rows[0, offset],
                tile_cols[0, offset],
                live,
            )
        )
    upper_rows = lax.psum_scatter(jnp.stack(blocks), "col", scatter_dimension=1, tiled=True)
    lowers = []
    for offset in range(1, offsets + 1):
        arrived = passed_along(upper_rows[offset], "sub", offset)
        lowers.append(jnp.transpose(arrived))
    coarse_lower = jnp.stack(lowers)[None]
    return (upper_rows[None], coarse_lower)


def solution(mesh):
    placed = (
        P("sub", "col"),
        P("sub", None, "col", None, None),
        P("sub", None, "col"),
        P("sub", None, "col"),
        P("sub", None),
    )
    return jax.shard_map(
        on_device,
        mesh=mesh,
        in_specs=placed,
        out_specs=(P("sub", None, "col", None), P("sub", None, None, "col")),
        check_vma=False,
    )
```

profile of v0, /device:TPU:128, one launch (start us, length us, event | category | flops | bytes accessed | tf_op | source)
XLA Modules:
  0.0 488.8 jit_solution(16397104175053290562)
XLA Ops:
  7.9 1.5 fusion.110
  10.1 16.9 %all-gather.2.cloned.1.call-done = bf16[4096,256]{1,0:T(8,128)(2,1)} async-done(((bf16[4096,128]{1,0:T(8,128)(2,1)}), bf16[4096,256]{1,0:T(8,128)(2,1)}) %all-gather.2.cloned.1.call-update) | async-done | bytes 2097168 | tf_op jit(solution)/shard_map/all_gather | solution.py:30
  27.0 6.7 %collective-permute-start = (bf16[4096,256]{1,0:T(8,128)(2,1)}, bf16[4096,256]{1,0:T(8,128)(2,1)}, u32[]{:S(2)}, u32[]{:S(2)}) collective-permute-start(bf16[4096,256]{1,0:T(8,128)(2,1)} %all-gather.2.cloned.1.call-done), channel_id=1, source_target_pairs={{2,0},{4,2},{6,4},{8,6},{10,8},{12,10},{14,12},{16,14},{18,16},{20... | collective-permute-start | bytes 6291464 | tf_op jit(solution)/shard_map/ppermute | solution.py:10
  33.7 2.8 collective-permute-start.1
  36.5 3.0 collective-permute-start.2
  39.5 2.5 collective-permute-start.3
  46.1 4.4 gather_fusion
  50.5 2.6 gather_fusion.1
  53.1 2.5 gather_fusion.2
  55.5 2.5 gather_fusion.4
  58.1 2.6 gather_fusion.6
  60.6 2.6 gather_fusion.8
  63.2 5.8 %fusion.95 = f32[5,256,256]{2,1,0:T(8,128)} fusion(bf16[48,128,256]{2,1,0:T(8,128)(2,1)} %gather_fusion, f32[48]{0:T(128)S(1)} %compare_convert_fusion.4, bf16[48,128,256]{2,1,0:T(8,128)(2,1)} %gather_fusion.1, bf16[1,5,48,128,128]{4,3,2,1,0:T(8,128)(2,1)} %param.6), kind=kOutput, calls=%fused_computation.54 | convolution fusion | flops 1211105280 | bytes 8126656 | tf_op jit(solution)/shard_map/pkr,pkc->rc/dot_general | solution.py:20
  69.0 129.6 %collective-permute-done = bf16[4096,256]{1,0:T(8,128)(2,1)} collective-permute-done((bf16[4096,256]{1,0:T(8,128)(2,1)}, bf16[4096,256]{1,0:T(8,128)(2,1)}, u32[]{:S(2)}, u32[]{:S(2)}) %collective-permute-start) | collective-permute-done | bytes 2097184 | tf_op jit(solution)/shard_map/ppermute | solution.py:10
  198.6 4.1 gather_fusion.3
  202.7 105.1 %collective-permute-done.1 = bf16[4096,256]{1,0:T(8,128)(2,1)} collective-permute-done((bf16[4096,256]{1,0:T(8,128)(2,1)}, bf16[4096,256]{1,0:T(8,128)(2,1)}, u32[]{:S(2)}, u32[]{:S(2)}) %collective-permute-start.1) | collective-permute-done | bytes 2097184 | tf_op jit(solution)/shard_map/ppermute | solution.py:10
  307.8 4.1 gather_fusion.5
  311.9 61.4 %collective-permute-done.2 = bf16[4096,256]{1,0:T(8,128)(2,1)} collective-permute-done((bf16[4096,256]{1,0:T(8,128)(2,1)}, bf16[4096,256]{1,0:T(8,128)(2,1)}, u32[]{:S(2)}, u32[]{:S(2)}) %collective-permute-start.2) | collective-permute-done | bytes 2097184 | tf_op jit(solution)/shard_map/ppermute | solution.py:10
  373.3 4.1 gather_fusion.7
  377.5 40.1 %collective-permute-done.3 = bf16[4096,256]{1,0:T(8,128)(2,1)} collective-permute-done((bf16[4096,256]{1,0:T(8,128)(2,1)}, bf16[4096,256]{1,0:T(8,128)(2,1)}, u32[]{:S(2)}, u32[]{:S(2)}) %collective-permute-start.3) | collective-permute-done | bytes 2097184 | tf_op jit(solution)/shard_map/ppermute | solution.py:10
  417.6 4.1 gather_fusion.9
  421.7 6.0 %fusion.85 = f32[5,256,256]{2,1,0:T(8,128)} fusion(f32[5,256,256]{2,1,0:T(8,128)} %fusion.95, bf16[48,128,256]{2,1,0:T(8,128)(2,1)} %gather_fusion.2, f32[48]{0:T(128)S(1)} %compare_convert_fusion.3, bf16[48,128,256]{2,1,0:T(8,128)(2,1)} %gather_fusion.3, bf16[1,5,48,128,128]{4,3,2,1,0:T(8,128)(2,1)} %param.6), kind=kOutput, calls=%fused_computation.52 | convolution fusion | flops 1211105280 | bytes 8126656 | tf_op jit(solution)/shard_map/pkr,pkc->rc/dot_general | solution.py:20
  427.7 4.9 fusion.75
  432.6 6.0 %fusion.65 = f32[5,256,256]{2,1,0:T(8,128)} fusion(f32[5,256,256]{2,1,0:T(8,128)} %fusion.75, bf16[48,128,256]{2,1,0:T(8,128)(2,1)} %gather_fusion.6, f32[48]{0:T(128)S(1)} %compare_convert_fusion.1, bf16[48,128,256]{2,1,0:T(8,128)(2,1)} %gather_fusion.7, bf16[1,5,48,128,128]{4,3,2,1,0:T(8,128)(2,1)} %param.6), kind=kOutput, calls=%fused_computation.48 | convolution fusion | flops 1211105280 | bytes 8126656 | tf_op jit(solution)/shard_map/pkr,pkc->rc/dot_general | solution.py:20
  438.6 4.9 fusion.55
  443.4 13.9 %reduce-scatter.2.cloned.1.call-done = f32[5,128,256]{2,1,0:T(8,128)} async-done(((f32[5,256,256]{2,1,0:T(8,128)}), f32[5,128,256]{2,1,0:T(8,128)}) %reduce-scatter.2.cloned.1.call-update) | async-done | bytes 655376 | tf_op jit(solution)/shard_map/reduce_scatter | solution.py:51
  458.4 3.4 collective-permute-start.4
  461.8 4.6 collective-permute-start.5
  466.4 4.3 collective-permute-start.6
  470.7 3.4 collective-permute-start.7
  474.8 2.8 collective-permute-done.6
  477.6 3.2 collective-permute-done.7
  (27 shorter events, 8.4 us)
Async XLA Ops:
  7.2 19.9 %all-gather.2.cloned.1.call-start = ((), (), s32[]{:S(2)}) async-start(), calls=%async_computation.1 | async-start | bytes 3145728 | tf_op jit(solution)/shard_map/all_gather | solution.py:30
  7.9 449.4 %reduce-scatter.2.cloned.1.call-start = ((), (), s32[]{:S(2)}) async-start(), calls=%async_computation.2 | async-start | bytes 1966080 | tf_op jit(solution)/shard_map/reduce_scatter | solution.py:51
  27.0 171.6 %collective-permute-start = (bf16[4096,256]{1,0:T(8,128)(2,1)}, bf16[4096,256]{1,0:T(8,128)(2,1)}, u32[]{:S(2)}, u32[]{:S(2)}) collective-permute-start(bf16[4096,256]{1,0:T(8,128)(2,1)} %all-gather.2.cloned.1.call-done), channel_id=1, source_target_pairs={{2,0},{4,2},{6,4},{8,6},{10,8},{12,10},{14,12},{16,14},{18,16},{20... | collective-permute-start | bytes 6291464 | tf_op jit(solution)/shard_map/ppermute | solution.py:10
  33.7 274.1 %collective-permute-start.1 = (bf16[4096,256]{1,0:T(8,128)(2,1)}, bf16[4096,256]{1,0:T(8,128)(2,1)}, u32[]{:S(2)}, u32[]{:S(2)}) collective-permute-start(bf16[4096,256]{1,0:T(8,128)(2,1)} %all-gather.2.cloned.1.call-done), channel_id=1, source_target_pairs={{4,0},{6,2},{8,4},{10,6},{12,8},{14,10},{16,12},{18,14},{20,16},{2... | collective-permute-start | bytes 6291464 | tf_op jit(solution)/shard_map/ppermute | solution.py:10
  36.5 336.8 %collective-permute-start.2 = (bf16[4096,256]{1,0:T(8,128)(2,1)}, bf16[4096,256]{1,0:T(8,128)(2,1)}, u32[]{:S(2)}, u32[]{:S(2)}) collective-permute-start(bf16[4096,256]{1,0:T(8,128)(2,1)} %all-gather.2.cloned.1.call-done), channel_id=1, source_target_pairs={{6,0},{8,2},{10,4},{12,6},{14,8},{16,10},{18,12},{20,14},{22,16},{... | collective-permute-start | bytes 6291464 | tf_op jit(solution)/shard_map/ppermute | solution.py:10
  39.5 378.1 %collective-permute-start.3 = (bf16[4096,256]{1,0:T(8,128)(2,1)}, bf16[4096,256]{1,0:T(8,128)(2,1)}, u32[]{:S(2)}, u32[]{:S(2)}) collective-permute-start(bf16[4096,256]{1,0:T(8,128)(2,1)} %all-gather.2.cloned.1.call-done), channel_id=1, source_target_pairs={{8,0},{10,2},{12,4},{14,6},{16,8},{18,10},{20,12},{22,14},{24,16},... | collective-permute-start | bytes 6291464 | tf_op jit(solution)/shard_map/ppermute | solution.py:10
  46.1 4.4 copy-start
  421.7 6.0 %copy-start.2 = (bf16[48,128,256]{2,1,0:T(8,128)(2,1)S(1)}, bf16[48,128,256]{2,1,0:T(8,128)(2,1)}, u32[]{:S(2)}) copy-start(bf16[48,128,256]{2,1,0:T(8,128)(2,1)} %gather_fusion.4) | copy-start | bytes 9437188
  432.6 6.0 %copy-start.1 = (bf16[48,128,256]{2,1,0:T(8,128)(2,1)S(1)}, bf16[48,128,256]{2,1,0:T(8,128)(2,1)}, u32[]{:S(2)}) copy-start(bf16[48,128,256]{2,1,0:T(8,128)(2,1)} %gather_fusion.8) | copy-start | bytes 9437188
  458.4 15.7 %collective-permute-start.4 = (f32[128,256]{1,0:T(8,128)S(1)}, f32[128,256]{1,0:T(8,128)S(1)}, u32[]{:S(2)}, u32[]{:S(2)}) collective-permute-start(f32[128,256]{1,0:T(8,128)S(1)} %get-tuple-element.6), channel_id=1, source_target_pairs={{0,2},{2,4},{4,6},{6,8},{8,10},{10,12},{12,14},{14,16},{16,18},{18... | collective-permute-start | bytes 393224 | tf_op jit(solution)/shard_map/ppermute | solution.py:10
  461.8 13.0 %collective-permute-start.5 = (f32[128,256]{1,0:T(8,128)S(1)}, f32[128,256]{1,0:T(8,128)S(1)}, u32[]{:S(2)}, u32[]{:S(2)}) collective-permute-start(f32[128,256]{1,0:T(8,128)S(1)} %get-tuple-element.9), channel_id=1, source_target_pairs={{0,4},{2,6},{4,8},{6,10},{8,12},{10,14},{12,16},{14,18},{16,20},{1... | collective-permute-start | bytes 393224 | tf_op jit(solution)/shard_map/ppermute | solution.py:10
  466.4 11.2 %collective-permute-start.6 = (f32[128,256]{1,0:T(8,128)S(1)}, f32[128,256]{1,0:T(8,128)S(1)}, u32[]{:S(2)}, u32[]{:S(2)}) collective-permute-start(f32[128,256]{1,0:T(8,128)S(1)} %get-tuple-element.8), channel_id=1, source_target_pairs={{0,6},{2,8},{4,10},{6,12},{8,14},{10,16},{12,18},{14,20},{16,22},{... | collective-permute-start | bytes 393224 | tf_op jit(solution)/shard_map/ppermute | solution.py:10
  470.7 10.2 %collective-permute-start.7 = (f32[128,256]{1,0:T(8,128)S(1)}, f32[128,256]{1,0:T(8,128)S(1)}, u32[]{:S(2)}, u32[]{:S(2)}) collective-permute-start(f32[128,256]{1,0:T(8,128)S(1)} %get-tuple-element.7), channel_id=1, source_target_pairs={{0,8},{2,10},{4,12},{6,14},{8,16},{10,18},{12,20},{14,22},{16,24},... | collective-permute-start | bytes 393224 | tf_op jit(solution)/shard_map/ppermute | solution.py:10
Sparse Core Ops, SparseCore 0:
  9.8 17.1 all-gather.1
  443.6 13.6 reduce-scatter.1
where the time goes:
time: 489 us
  waiting for transfers between devices  374 us (76%)
  local copies, waits for them, and re-layouts  37.2 us (8%)
  starting transfers between devices  30.6 us (6%)
  matrix products  27.5 us (6%)
  between operations  14.2 us (3%)
    ppermute x8, waiting for transfers between devices, passed_along(): return lax.ppermute(block, axis, route)  343 us
    ppermute x8, starting transfers between devices, passed_along(): return lax.ppermute(block, axis, route)  30.6 us
    dot_general x5, matrix products, form_block(): jnp.einsum('pkr,pkc->rc', own_tiles[rows_idx], applied, preferred_element...  27.5 us
    gather x5, local copies, waits for them, and re-layouts, form_block(): far_tiles[cols_idx]  19.1 us
    all_gather x1, waiting for transfers between devices, on_device(): own_full = lax.all_gather(prolong, 'col', axis=1, tiled=True)  16.9 us
    gather x5, local copies, waits for them, and re-layouts, form_block(): own_tiles[rows_idx]  14.5 us
    reduce_scatter x1, waiting for transfers between devices, on_device(): lax.psum_scatter(jnp.stack(blocks), 'col', scatter_dimension=1, tiled=True)  13.9 us
  transfers between devices with their start and end apart: 10, of which 9 were waited for; matrix products, arithmetic and copies ran while one was open for 8% of the time, Pallas kernels for 0%

commit v1 on v0

v1 whole, which is shorter than its diff:
```python
import functools

import jax
import jax.numpy as jnp
from jax import lax
from jax.experimental import pallas as pl
from jax.experimental.pallas import tpu as pltpu
from jax.sharding import PartitionSpec as P

NSUB = 128
ROW = 4
GROUP = 4


def shift(value, distance):
    route = [((s + distance) % NSUB, s) for s in range(NSUB)]
    return lax.ppermute(value, "sub", route)


def swap(value):
    return lax.ppermute(value, "col", [(0, 1), (1, 0)])


def weights_kernel(rows, cols, live, p0, p1, tiles, out, pt, acc):
    o = pl.program_id(0)
    nt = acc.shape[0]
    edge = tiles.shape[-1]

    @pl.when(o == 0)
    def _():
        for t in range(nt):
            pt[t, :edge, :] = p0[t * edge : (t + 1) * edge, :].T
            pt[t, edge:, :] = p1[t * edge : (t + 1) * edge, :].T

    acc[...] = jnp.zeros_like(acc)
    n = live[o]

    def group(g, carry):
        parts = []
        for j in range(GROUP):
            p = g * GROUP + j
            part = jnp.dot(pt[rows[o, p]], tiles[0, p], preferred_element_type=jnp.float32)
            parts.append(jnp.where(p < n, part, 0.0))
        for j in range(GROUP):
            c = cols[o, g * GROUP + j]
            acc[c] += parts[j]
        return carry

    lax.fori_loop(0, (n + GROUP - 1) // GROUP, group, 0)
    for t in range(nt):
        out[0, :, t * edge : (t + 1) * edge] = acc[t].astype(out.dtype)


def weights(rows, cols, live, p0, p1, tiles):
    offsets, slots, edge, _ = tiles.shape
    fine = p0.shape[0]
    nt = fine // edge
    whole = lambda o, *_: (0, 0)
    return pl.pallas_call(
        weights_kernel,
        grid_spec=pltpu.PrefetchScalarGridSpec(
            num_scalar_prefetch=3,
            grid=(offsets,),
            in_specs=[
                pl.BlockSpec((fine, edge), whole),
                pl.BlockSpec((fine, edge), whole),
                pl.BlockSpec((1, slots, edge, edge), lambda o, *_: (o, 0, 0, 0)),
            ],
            out_specs=pl.BlockSpec((1, 2 * edge, fine), lambda o, *_: (o, 0, 0)),
            scratch_shapes=[
                pltpu.VMEM((nt, 2 * edge, edge), jnp.bfloat16),
                pltpu.VMEM((nt, 2 * edge, edge), jnp.float32),
            ],
        ),
        out_shape=jax.ShapeDtypeStruct((offsets, 2 * edge, fine), jnp.bfloat16),
        compiler_params=pltpu.CompilerParams(vmem_limit_bytes=32 * 1024 * 1024),
        cost_estimate=pl.CostEstimate(
            flops=offsets * slots * 4 * edge**3, bytes_accessed=20 * 2**20, transcendentals=0
        ),
    )(rows, cols, live, p0, p1, tiles)


def on_device(prolong, tiles, tile_rows, tile_cols, counts):
    slots = tiles.shape[2]
    offsets = tiles.shape[1]
    fine = prolong.shape[0]
    half = fine // 2
    core = lax.axis_index("col")
    sub = lax.axis_index("sub")
    pa, pb = prolong[:half], prolong[half:]

    away = [(s, (s - 1) % NSUB) for s in range(NSUB) if s % ROW != 0]
    wrap = [(s, s + ROW - 1) for s in range(NSUB) if s % ROW == 0]
    y_a = shift(pa, 4)
    a_a = lax.ppermute(pa, "sub", away)
    y_b = shift(pb, 4)
    a_b = lax.ppermute(pb, "sub", away)
    a_a = a_a + lax.ppermute(y_a, "sub", wrap)
    a_b = a_b + lax.ppermute(y_b, "sub", wrap)
    b_a = shift(y_a, -1)
    b_b = shift(y_b, -1)
    d_a = shift(a_a, 1)
    d_b = shift(b_b, -1)
    panels = [(pa, pb), (a_a, a_b), (d_a, d_b), (b_a, b_b), (y_a, y_b)]

    other = swap(prolong)
    first = jnp.where(core == 0, prolong, other)
    second = jnp.where(core == 0, other, prolong)
    live = jnp.clip(counts[0] - core * slots, 0, slots)
    live = jnp.where(sub + jnp.arange(offsets) < NSUB, live, 0).astype(jnp.int32)
    mine = weights(tile_rows[0], tile_cols[0], live, first, second, tiles[0])
    theirs = swap(mine)

    def dot(w, p):
        return jnp.dot(w, p, preferred_element_type=jnp.float32)

    uppers = []
    lowers = []
    width = prolong.shape[1]
    for o in range(offsets):
        a, b = panels[o]
        c = (dot(mine[o, :, :half], a) + dot(theirs[o, :, :half], a)) + (
            dot(mine[o, :, half:], b) + dot(theirs[o, :, half:], b)
        )
        keep = jnp.where(core == 0, c[:width], c[width:])
        give = jnp.where(core == 0, c[width:], c[:width])
        got = swap(give)
        upper = jnp.concatenate(
            [jnp.where(core == 0, keep, got), jnp.where(core == 0, got, keep)], axis=1
        )
        uppers.append(upper)
        if o > 0:
            arrived = lax.ppermute(upper, "sub", [(s, s + o) for s in range(NSUB - o)])
            lowers.append(arrived.T)
    return jnp.stack(uppers)[None], jnp.stack(lowers)[None]


def solution(mesh):
    placed = (
        P("sub", "col"),
        P("sub", None, "col", None, None),
        P("sub", None, "col"),
        P("sub", None, "col"),
        P("sub", None),
    )
    return jax.shard_map(
        on_device,
        mesh=mesh,
        in_specs=placed,
        out_specs=(P("sub", None, "col", None), P("sub", None, None, "col")),
        check_vma=False,
    )
```

time: 489 us -> 126 us (0.26)
  waiting for transfers between devices: 374 us -> 56.4 us
  local copies, waits for them, and re-layouts: 37.2 us -> 5.07 us
  Pallas kernels: 0 us -> 18.9 us
  matrix products: 27.5 us -> 9.87 us
  between operations: 14.2 us -> 1.15 us
    ppermute x8 -> x21, waiting for transfers between devices: 343 us -> 56.4 us  [the longest x6 34.4 us: shift(): return lax.ppermute(value, 'sub', route)]
    gather x10 -> x0, local copies, waits for them, and re-layouts: 33.6 us -> none  [the longest x5 19.1 us: form_block(): far_tiles[cols_idx]]
    pallas_call x0 -> x1, Pallas kernels: none -> 18.9 us  [weights(): pl.pallas_call(weights_kernel, grid_spec=pltpu.PrefetchScalarGridSpec(num...]
    dot_general x5 -> x20, matrix products: 27.5 us -> 9.87 us  [dot(): return jnp.dot(w, p, preferred_element_type=jnp.float32)]
    all_gather x1 -> x0, waiting for transfers between devices: 16.9 us -> none  [on_device(): own_full = lax.all_gather(prolong, 'col', axis=1, tiled=True)]
    reduce_scatter x1 -> x0, waiting for transfers between devices: 13.9 us -> none  [on_device(): lax.psum_scatter(jnp.stack(blocks), 'col', scatter_dimension=1, tiled=True)]
    ppermute x8 -> x21, starting transfers between devices: 30.6 us -> 31.2 us  [the longest x4 8.94 us: on_device(): arrived = lax.ppermute(upper, 'sub', [(s, s + o) for s in range(NSUB - o)])]
  transfers between devices with their start and end apart: 10 -> 21, of which waited for: 9 -> 11; matrix products, arithmetic and copies ran while one was open for 8% -> 10% of each run, Pallas kernels for 0% -> 0%
where the time goes in v1:
time: 126 us
  waiting for transfers between devices  56.4 us (45%)
  starting transfers between devices  31.2 us (25%)
  Pallas kernels  18.9 us (15%)
  matrix products  9.87 us (8%)
  local copies, waits for them, and re-layouts  5.07 us (4%)
  other arithmetic  3.31 us (3%)
    ppermute x6, waiting for transfers between devices, shift(): return lax.ppermute(value, 'sub', route)  34.4 us
    pallas_call x1, Pallas kernels, weights(): pl.pallas_call(weights_kernel, grid_spec=pltpu.PrefetchScalarGridSpec(num...  18.9 us
    ppermute x4, waiting for transfers between devices, on_device(): arrived = lax.ppermute(upper, 'sub', [(s, s + o) for s in range(NSUB - o)])  11 us
    dot_general x20, matrix products, dot(): return jnp.dot(w, p, preferred_element_type=jnp.float32)  9.87 us
    ppermute x4, starting transfers between devices, on_device(): arrived = lax.ppermute(upper, 'sub', [(s, s + o) for s in range(NSUB - o)])  8.94 us
    ppermute x6, starting transfers between devices, shift(): return lax.ppermute(value, 'sub', route)  8.88 us
    ppermute x1, waiting for transfers between devices, on_device(): a_b = a_b + lax.ppermute(y_b, 'sub', wrap)  7.07 us
    unnamed x6, local copies, waits for them, and re-layouts  5 us
  transfers between devices with their start and end apart: 21, of which 11 were waited for; matrix products, arithmetic and copies ran while one was open for 10% of the time, Pallas kernels for 0%

profile of v1, /device:TPU:128, one launch (start us, length us, event | category | flops | bytes accessed | tf_op | source)
XLA Modules:
  0.0 125.9 jit_solution(15900518065167880187)
XLA Ops:
  0.7 0.7 compare_select_fusion.live
  1.4 0.7 copy_bitcast_fusion
  2.1 1.5 %collective-permute-done = bf16[4096,128]{1,0:T(8,128)(2,1)S(1)} collective-permute-done((bf16[4096,128]{1,0:T(8,128)(2,1)}, bf16[4096,128]{1,0:T(8,128)(2,1)S(1)}, u32[]{:S(2)}, u32[]{:S(2)}) %collective-permute-start) | collective-permute-done | bytes 1048608 | tf_op jit(solution)/shard_map/ppermute | solution.py:21
  3.6 1.5 %broadcast_select_fusion = (bf16[4096,128]{1,0:T(8,128)(2,1)S(1)}, bf16[4096,128]{1,0:T(8,128)(2,1)S(1)}) fusion(bf16[4096,128]{1,0:T(8,128)(2,1)S(1)} %collective-permute-done, bf16[4096,128]{1,0:T(8,128)(2,1)} %param.5, pred[]{:T(512)S(6)} %eq.2), kind=kLoop, calls=%fused_computation.45 | loop fusion | flops 1048576 | bytes 4194305 | tf_op jit(solution)/shard_map/jit(_where)/select_n | solution.py:108
  5.1 3.2 %copy-done = bf16[1,5,48,128,128]{4,3,2,1,0:T(8,128)(2,1)S(1)} copy-done((bf16[1,5,48,128,128]{4,3,2,1,0:T(8,128)(2,1)S(1)}, bf16[1,5,48,128,128]{4,3,2,1,0:T(8,128)(2,1)}, u32[]{:S(2)}) %copy-start) | copy-done | bytes 7864344
  8.3 18.9 %shard_map.68 = bf16[5,256,4096]{2,1,0:T(8,128)(2,1)S(1)} custom-call(s32[5,48]{1,0:T(8,128)S(1)} %get-tuple-element.19.rows, s32[5,48]{1,0:T(8,128)S(1)} %get-tuple-element.18.cols, s32[5]{0:T(128)S(1)} %compare_select_fusion.live, bf16[4096,128]{1,0:T(8,128)(2,1)S(1)} %get-tuple-element.5.p0, bf16[4096,128]{1,0:T(8,128)(2,1)S(1)} %get-tuple-element.4.p1, ...), custom_call_target="tpu_custom_call" | custom-call | flops 2013265920 | bytes 20971520 | tf_op jit(solution)/shard_map/pallas_call | solution.py:59
  27.3 2.0 %collective-permute-start.4 = (bf16[2048,128]{1,0:T(8,128)(2,1)S(1)}, bf16[2048,128]{1,0:T(8,128)(2,1)S(1)}, u32[]{:S(2)}, u32[]{:S(2)}) collective-permute-start(bf16[2048,128]{1,0:T(8,128)(2,1)S(1)} %get-tuple-element.6), channel_id=1, source_target_pairs={{8,0},{10,2},{12,4},{14,6},{16,8},{18,10},{20,12},{22,14},{24,16},... | collective-permute-start | bytes 1572872 | tf_op jit(solution)/shard_map/ppermute | solution.py:17
  29.3 0.5 collective-permute-start.7
  29.8 1.3 %collective-permute-start.3 = (bf16[2048,128]{1,0:T(8,128)(2,1)S(1)}, bf16[2048,128]{1,0:T(8,128)(2,1)S(1)}, u32[]{:S(2)}, u32[]{:S(2)}) collective-permute-start(bf16[2048,128]{1,0:T(8,128)(2,1)S(1)} %get-tuple-element.6), channel_id=1, source_target_pairs={{2,0},{4,2},{6,4},{10,8},{12,10},{14,12},{18,16},{20,18},{22,20},{... | collective-permute-start | bytes 1572872 | tf_op jit(solution)/shard_map/ppermute | solution.py:95
  31.1 11.0 %collective-permute-done.4 = bf16[2048,128]{1,0:T(8,128)(2,1)S(1)} collective-permute-done((bf16[2048,128]{1,0:T(8,128)(2,1)S(1)}, bf16[2048,128]{1,0:T(8,128)(2,1)S(1)}, u32[]{:S(2)}, u32[]{:S(2)}) %collective-permute-start.4) | collective-permute-done | bytes 524320 | tf_op jit(solution)/shard_map/ppermute | solution.py:17
  42.1 4.5 %collective-permute-start.5 = (bf16[2048,128]{1,0:T(8,128)(2,1)S(1)}, bf16[2048,128]{1,0:T(8,128)(2,1)S(1)}, u32[]{:S(2)}, u32[]{:S(2)}) collective-permute-start(bf16[2048,128]{1,0:T(8,128)(2,1)S(1)} %collective-permute-done.4), channel_id=1, source_target_pairs={{0,6},{8,14},{16,22},{24,30},{32,38},{40,46},{48,54},{56,62},{64,7... | collective-permute-start | bytes 1572872 | tf_op jit(solution)/shard_map/ppermute | solution.py:98
  46.7 1.3 %collective-permute-start.6 = (bf16[2048,128]{1,0:T(8,128)(2,1)S(1)}, bf16[2048,128]{1,0:T(8,128)(2,1)S(1)}, u32[]{:S(2)}, u32[]{:S(2)}) collective-permute-start(bf16[2048,128]{1,0:T(8,128)(2,1)S(1)} %get-tuple-element.7), channel_id=1, source_target_pairs={{2,0},{4,2},{6,4},{10,8},{12,10},{14,12},{18,16},{20,18},{22,20},{... | collective-permute-start | bytes 1572872 | tf_op jit(solution)/shard_map/ppermute | solution.py:97
  48.0 5.0 %collective-permute-done.7 = bf16[2048,128]{1,0:T(8,128)(2,1)S(1)} collective-permute-done((bf16[2048,128]{1,0:T(8,128)(2,1)S(1)}, bf16[2048,128]{1,0:T(8,128)(2,1)S(1)}, u32[]{:S(2)}, u32[]{:S(2)}) %collective-permute-start.7) | collective-permute-done | bytes 524320 | tf_op jit(solution)/shard_map/ppermute | solution.py:17
  53.0 1.3 %collective-permute-start.11 = (bf16[2048,128]{1,0:T(8,128)(2,1)S(1)}, bf16[2048,128]{1,0:T(8,128)(2,1)S(1)}, u32[]{:S(2)}, u32[]{:S(2)}) collective-permute-start(bf16[2048,128]{1,0:T(8,128)(2,1)S(1)} %collective-permute-done.7), channel_id=1, source_target_pairs={{254,0},{0,2},{2,4},{4,6},{6,8},{8,10},{10,12},{12,14},{14,16},{16... | collective-permute-start | bytes 1572872 | tf_op jit(solution)/shard_map/ppermute | solution.py:17
  54.2 4.5 %collective-permute-start.8 = (bf16[2048,128]{1,0:T(8,128)(2,1)S(1)}, bf16[2048,128]{1,0:T(8,128)(2,1)S(1)}, u32[]{:S(2)}, u32[]{:S(2)}) collective-permute-start(bf16[2048,128]{1,0:T(8,128)(2,1)S(1)} %collective-permute-done.7), channel_id=1, source_target_pairs={{0,6},{8,14},{16,22},{24,30},{32,38},{40,46},{48,54},{56,62},{64,7... | collective-permute-start | bytes 1572872 | tf_op jit(solution)/shard_map/ppermute | solution.py:99
  59.0 2.5 %collective-permute-done.6 = bf16[2048,128]{1,0:T(8,128)(2,1)S(1)} collective-permute-done((bf16[2048,128]{1,0:T(8,128)(2,1)S(1)}, bf16[2048,128]{1,0:T(8,128)(2,1)S(1)}, u32[]{:S(2)}, u32[]{:S(2)}) %collective-permute-start.6) | collective-permute-done | bytes 524320 | tf_op jit(solution)/shard_map/ppermute | solution.py:97
  61.4 5.0 %collective-permute-start.10 = (bf16[2048,128]{1,0:T(8,128)(2,1)S(1)}, bf16[2048,128]{1,0:T(8,128)(2,1)S(1)}, u32[]{:S(2)}, u32[]{:S(2)}) collective-permute-start(bf16[2048,128]{1,0:T(8,128)(2,1)S(1)} %add.62), channel_id=1, source_target_pairs={{2,0},{4,2},{6,4},{8,6},{10,8},{12,10},{14,12},{16,14},{18,16},{20... | collective-permute-start | bytes 1572872 | tf_op jit(solution)/shard_map/ppermute | solution.py:17
  66.5 7.1 %collective-permute-done.11 = bf16[2048,128]{1,0:T(8,128)(2,1)S(1)} collective-permute-done((bf16[2048,128]{1,0:T(8,128)(2,1)S(1)}, bf16[2048,128]{1,0:T(8,128)(2,1)S(1)}, u32[]{:S(2)}, u32[]{:S(2)}) %collective-permute-start.11) | collective-permute-done | bytes 524320 | tf_op jit(solution)/shard_map/ppermute | solution.py:17
  73.6 7.1 %collective-permute-done.8 = bf16[2048,128]{1,0:T(8,128)(2,1)S(1)} collective-permute-done((bf16[2048,128]{1,0:T(8,128)(2,1)S(1)}, bf16[2048,128]{1,0:T(8,128)(2,1)S(1)}, u32[]{:S(2)}, u32[]{:S(2)}) %collective-permute-start.8) | collective-permute-done | bytes 524320 | tf_op jit(solution)/shard_map/ppermute | solution.py:99
  83.8 11.3 %collective-permute-done.12 = bf16[2048,128]{1,0:T(8,128)(2,1)S(1)} collective-permute-done((bf16[2048,128]{1,0:T(8,128)(2,1)S(1)}, bf16[2048,128]{1,0:T(8,128)(2,1)S(1)}, u32[]{:S(2)}, u32[]{:S(2)}) %collective-permute-start.12) | collective-permute-done | bytes 524320 | tf_op jit(solution)/shard_map/ppermute | solution.py:17
  98.4 0.6 collective-permute-start.15
  103.1 0.6 collective-permute-start.2
  103.8 1.9 %collective-permute-start.17 = (f32[128,256]{0,1:T(8,128)S(1)}, f32[128,256]{0,1:T(8,128)S(1)}, u32[]{:S(2)}, u32[]{:S(2)}) collective-permute-start(f32[128,256]{0,1:T(8,128)S(1)} %pad_maximum_fusion), channel_id=1, source_target_pairs={{0,2},{2,4},{4,6},{6,8},{8,10},{10,12},{12,14},{14,16},{16,18},{18... | collective-permute-start | bytes 393224 | tf_op jit(solution)/shard_map/ppermute | solution.py:133
  105.7 1.9 %collective-permute-start.18 = (f32[128,256]{0,1:T(8,128)S(1)}, f32[128,256]{0,1:T(8,128)S(1)}, u32[]{:S(2)}, u32[]{:S(2)}) collective-permute-start(f32[128,256]{0,1:T(8,128)S(1)} %pad_maximum_fusion.1), channel_id=1, source_target_pairs={{0,4},{2,6},{4,8},{6,10},{8,12},{10,14},{12,16},{14,18},{16,20},{1... | collective-permute-start | bytes 393224 | tf_op jit(solution)/shard_map/ppermute | solution.py:133
  107.7 2.5 %collective-permute-start.19 = (f32[128,256]{0,1:T(8,128)S(1)}, f32[128,256]{0,1:T(8,128)S(1)}, u32[]{:S(2)}, u32[]{:S(2)}) collective-permute-start(f32[128,256]{0,1:T(8,128)S(1)} %pad_maximum_fusion.2), channel_id=1, source_target_pairs={{0,6},{2,8},{4,10},{6,12},{8,14},{10,16},{12,18},{14,20},{16,22},{... | collective-permute-start | bytes 393224 | tf_op jit(solution)/shard_map/ppermute | solution.py:133
  110.2 2.6 %collective-permute-start.20 = (f32[128,256]{0,1:T(8,128)S(1)}, f32[128,256]{0,1:T(8,128)S(1)}, u32[]{:S(2)}, u32[]{:S(2)}) collective-permute-start(f32[128,256]{0,1:T(8,128)S(1)} %pad_maximum_fusion.3), channel_id=1, source_target_pairs={{0,8},{2,10},{4,12},{6,14},{8,16},{10,18},{12,20},{14,22},{16,24},... | collective-permute-start | bytes 393224 | tf_op jit(solution)/shard_map/ppermute | solution.py:133
  113.0 1.1 copy.7
  114.1 3.9 %collective-permute-done.17 = f32[128,256]{0,1:T(8,128)S(1)} collective-permute-done((f32[128,256]{0,1:T(8,128)S(1)}, f32[128,256]{0,1:T(8,128)S(1)}, u32[]{:S(2)}, u32[]{:S(2)}) %collective-permute-start.17) | collective-permute-done | bytes 131104 | tf_op jit(solution)/shard_map/ppermute | solution.py:133
  118.0 2.7 %collective-permute-done.18 = f32[128,256]{0,1:T(8,128)S(1)} collective-permute-done((f32[128,256]{0,1:T(8,128)S(1)}, f32[128,256]{0,1:T(8,128)S(1)}, u32[]{:S(2)}, u32[]{:S(2)}) %collective-permute-start.18) | collective-permute-done | bytes 131104 | tf_op jit(solution)/shard_map/ppermute | solution.py:133
  120.6 3.8 %collective-permute-done.19 = f32[128,256]{0,1:T(8,128)S(1)} collective-permute-done((f32[128,256]{0,1:T(8,128)S(1)}, f32[128,256]{0,1:T(8,128)S(1)}, u32[]{:S(2)}, u32[]{:S(2)}) %collective-permute-start.19) | collective-permute-done | bytes 131104 | tf_op jit(solution)/shard_map/ppermute | solution.py:133
  124.4 0.6 collective-permute-done.20
  125.1 0.8 maximum_bitcast_fusion
  (61 shorter events, 11.1 us)
Async XLA Ops:
  0.6 3.0 %collective-permute-start = (bf16[4096,128]{1,0:T(8,128)(2,1)}, bf16[4096,128]{1,0:T(8,128)(2,1)S(1)}, u32[]{:S(2)}, u32[]{:S(2)}) collective-permute-start(bf16[4096,128]{1,0:T(8,128)(2,1)} %param.5), channel_id=1, source_target_pairs={{0,1},{1,0},{2,3},{3,2},{4,5},{5,4},{6,7},{7,6},{8,9},{9,8},{10,11... | collective-permute-start | bytes 3145736 | tf_op jit(solution)/shard_map/ppermute | solution.py:21
  3.6 23.7 %copy-start.1 = (bf16[4096,128]{1,0:T(8,128)(2,1)S(1)}, bf16[4096,128]{1,0:T(8,128)(2,1)}, u32[]{:S(2)}) copy-start(bf16[4096,128]{1,0:T(8,128)(2,1)} %param.5) | copy-start | bytes 3145732
  5.0 3.2 %copy-start = (bf16[1,5,48,128,128]{4,3,2,1,0:T(8,128)(2,1)S(1)}, bf16[1,5,48,128,128]{4,3,2,1,0:T(8,128)(2,1)}, u32[]{:S(2)}) copy-start(bf16[1,5,48,128,128]{4,3,2,1,0:T(8,128)(2,1)} %param.6) | copy-start | bytes 23592964
  27.2 53.5 %collective-permute-start.1 = (bf16[5,256,4096]{2,1,0:T(8,128)(2,1)S(1)}, bf16[5,256,4096]{2,1,0:T(8,128)(2,1)S(1)}, u32[]{:S(2)}, u32[]{:S(2)}) collective-permute-start(bf16[5,256,4096]{2,1,0:T(8,128)(2,1)S(1)} %shard_map.68), channel_id=1, source_target_pairs={{0,1},{1,0},{2,3},{3,2},{4,5},{5,4},{6,7},{7,6},{8,9},{9,8},{10,11... | collective-permute-start | bytes 31457288 | tf_op jit(solution)/shard_map/ppermute | solution.py:21
  27.3 14.8 %collective-permute-start.4 = (bf16[2048,128]{1,0:T(8,128)(2,1)S(1)}, bf16[2048,128]{1,0:T(8,128)(2,1)S(1)}, u32[]{:S(2)}, u32[]{:S(2)}) collective-permute-start(bf16[2048,128]{1,0:T(8,128)(2,1)S(1)} %get-tuple-element.6), channel_id=1, source_target_pairs={{8,0},{10,2},{12,4},{14,6},{16,8},{18,10},{20,12},{22,14},{24,16},... | collective-permute-start | bytes 1572872 | tf_op jit(solution)/shard_map/ppermute | solution.py:17
  29.3 23.7 %collective-permute-start.7 = (bf16[2048,128]{1,0:T(8,128)(2,1)S(1)}, bf16[2048,128]{1,0:T(8,128)(2,1)S(1)}, u32[]{:S(2)}, u32[]{:S(2)}) collective-permute-start(bf16[2048,128]{1,0:T(8,128)(2,1)S(1)} %get-tuple-element.7), channel_id=1, source_target_pairs={{8,0},{10,2},{12,4},{14,6},{16,8},{18,10},{20,12},{22,14},{24,16},... | collective-permute-start | bytes 1572872 | tf_op jit(solution)/shard_map/ppermute | solution.py:17
  29.8 24.4 %collective-permute-start.3 = (bf16[2048,128]{1,0:T(8,128)(2,1)S(1)}, bf16[2048,128]{1,0:T(8,128)(2,1)S(1)}, u32[]{:S(2)}, u32[]{:S(2)}) collective-permute-start(bf16[2048,128]{1,0:T(8,128)(2,1)S(1)} %get-tuple-element.6), channel_id=1, source_target_pairs={{2,0},{4,2},{6,4},{10,8},{12,10},{14,12},{18,16},{20,18},{22,20},{... | collective-permute-start | bytes 1572872 | tf_op jit(solution)/shard_map/ppermute | solution.py:95
  42.1 16.6 %collective-permute-start.5 = (bf16[2048,128]{1,0:T(8,128)(2,1)S(1)}, bf16[2048,128]{1,0:T(8,128)(2,1)S(1)}, u32[]{:S(2)}, u32[]{:S(2)}) collective-permute-start(bf16[2048,128]{1,0:T(8,128)(2,1)S(1)} %collective-permute-done.4), channel_id=1, source_target_pairs={{0,6},{8,14},{16,22},{24,30},{32,38},{40,46},{48,54},{56,62},{64,7... | collective-permute-start | bytes 1572872 | tf_op jit(solution)/shard_map/ppermute | solution.py:98
  46.7 14.7 %collective-permute-start.6 = (bf16[2048,128]{1,0:T(8,128)(2,1)S(1)}, bf16[2048,128]{1,0:T(8,128)(2,1)S(1)}, u32[]{:S(2)}, u32[]{:S(2)}) collective-permute-start(bf16[2048,128]{1,0:T(8,128)(2,1)S(1)} %get-tuple-element.7), channel_id=1, source_target_pairs={{2,0},{4,2},{6,4},{10,8},{12,10},{14,12},{18,16},{20,18},{22,20},{... | collective-permute-start | bytes 1572872 | tf_op jit(solution)/shard_map/ppermute | solution.py:97
  53.0 20.6 %collective-permute-start.11 = (bf16[2048,128]{1,0:T(8,128)(2,1)S(1)}, bf16[2048,128]{1,0:T(8,128)(2,1)S(1)}, u32[]{:S(2)}, u32[]{:S(2)}) collective-permute-start(bf16[2048,128]{1,0:T(8,128)(2,1)S(1)} %collective-permute-done.7), channel_id=1, source_target_pairs={{254,0},{0,2},{2,4},{4,6},{6,8},{8,10},{10,12},{12,14},{14,16},{16... | collective-permute-start | bytes 1572872 | tf_op jit(solution)/shard_map/ppermute | solution.py:17
  54.2 26.4 %collective-permute-start.8 = (bf16[2048,128]{1,0:T(8,128)(2,1)S(1)}, bf16[2048,128]{1,0:T(8,128)(2,1)S(1)}, u32[]{:S(2)}, u32[]{:S(2)}) collective-permute-start(bf16[2048,128]{1,0:T(8,128)(2,1)S(1)} %collective-permute-done.7), channel_id=1, source_target_pairs={{0,6},{8,14},{16,22},{24,30},{32,38},{40,46},{48,54},{56,62},{64,7... | collective-permute-start | bytes 1572872 | tf_op jit(solution)/shard_map/ppermute | solution.py:99
  58.7 38.7 %collective-permute-start.14 = (bf16[2048,128]{1,0:T(8,128)(2,1)S(1)}, bf16[2048,128]{1,0:T(8,128)(2,1)S(1)}, u32[]{:S(2)}, u32[]{:S(2)}) collective-permute-start(bf16[2048,128]{1,0:T(8,128)(2,1)S(1)} %collective-permute-done.4), channel_id=1, source_target_pairs={{254,0},{0,2},{2,4},{4,6},{6,8},{8,10},{10,12},{12,14},{14,16},{16... | collective-permute-start | bytes 1572872 | tf_op jit(solution)/shard_map/ppermute | solution.py:17
  61.4 21.4 %collective-permute-start.10 = (bf16[2048,128]{1,0:T(8,128)(2,1)S(1)}, bf16[2048,128]{1,0:T(8,128)(2,1)S(1)}, u32[]{:S(2)}, u32[]{:S(2)}) collective-permute-start(bf16[2048,128]{1,0:T(8,128)(2,1)S(1)} %add.62), channel_id=1, source_target_pairs={{2,0},{4,2},{6,4},{8,6},{10,8},{12,10},{14,12},{16,14},{18,16},{20... | collective-permute-start | bytes 1572872 | tf_op jit(solution)/shard_map/ppermute | solution.py:17
  73.6 21.5 %collective-permute-start.12 = (bf16[2048,128]{1,0:T(8,128)(2,1)S(1)}, bf16[2048,128]{1,0:T(8,128)(2,1)S(1)}, u32[]{:S(2)}, u32[]{:S(2)}) collective-permute-start(bf16[2048,128]{1,0:T(8,128)(2,1)S(1)} %collective-permute-done.11), channel_id=1, source_target_pairs={{254,0},{0,2},{2,4},{4,6},{6,8},{8,10},{10,12},{12,14},{14,16},{16... | collective-permute-start | bytes 1572872 | tf_op jit(solution)/shard_map/ppermute | solution.py:17
  82.7 21.0 %collective-permute-start.9 = (f32[128,128]{0,1:T(8,128)S(1)}, f32[128,128]{0,1:T(8,128)S(1)}, u32[]{:S(2)}, u32[]{:S(2)}) collective-permute-start(f32[128,128]{0,1:T(8,128)S(1)} %slice_select_fusion.6), channel_id=1, source_target_pairs={{0,1},{1,0},{2,3},{3,2},{4,5},{5,4},{6,7},{7,6},{8,9},{9,8},{10,11... | collective-permute-start | bytes 196616 | tf_op jit(solution)/shard_map/ppermute | solution.py:21
  96.1 9.6 %collective-permute-start.13 = (f32[128,128]{0,1:T(8,128)S(1)}, f32[128,128]{0,1:T(8,128)S(1)}, u32[]{:S(2)}, u32[]{:S(2)}) collective-permute-start(f32[128,128]{0,1:T(8,128)S(1)} %slice_select_fusion.4), channel_id=1, source_target_pairs={{0,1},{1,0},{2,3},{3,2},{4,5},{5,4},{6,7},{7,6},{8,9},{9,8},{10,11... | collective-permute-start | bytes 196616 | tf_op jit(solution)/shard_map/ppermute | solution.py:21
  98.4 9.3 %collective-permute-start.15 = (f32[128,128]{0,1:T(8,128)S(1)}, f32[128,128]{0,1:T(8,128)S(1)}, u32[]{:S(2)}, u32[]{:S(2)}) collective-permute-start(f32[128,128]{0,1:T(8,128)S(1)} %slice_select_fusion.2), channel_id=1, source_target_pairs={{0,1},{1,0},{2,3},{3,2},{4,5},{5,4},{6,7},{7,6},{8,9},{9,8},{10,11... | collective-permute-start | bytes 196616 | tf_op jit(solution)/shard_map/ppermute | solution.py:21
  101.0 9.2 %collective-permute-start.16 = (f32[128,128]{0,1:T(8,128)S(1)}, f32[128,128]{0,1:T(8,128)S(1)}, u32[]{:S(2)}, u32[]{:S(2)}) collective-permute-start(f32[128,128]{0,1:T(8,128)S(1)} %slice_select_fusion), channel_id=1, source_target_pairs={{0,1},{1,0},{2,3},{3,2},{4,5},{5,4},{6,7},{7,6},{8,9},{9,8},{10,11... | collective-permute-start | bytes 196616 | tf_op jit(solution)/shard_map/ppermute | solution.py:21
  103.1 9.8 %collective-permute-start.2 = (f32[128,128]{0,1:T(8,128)S(1)}, f32[128,128]{0,1:T(8,128)S(1)}, u32[]{:S(2)}, u32[]{:S(2)}) collective-permute-start(f32[128,128]{0,1:T(8,128)S(1)} %slice_select_fusion.8), channel_id=1, source_target_pairs={{0,1},{1,0},{2,3},{3,2},{4,5},{5,4},{6,7},{7,6},{8,9},{9,8},{10,11... | collective-permute-start | bytes 196616 | tf_op jit(solution)/shard_map/ppermute | solution.py:21
  103.8 14.2 %collective-permute-start.17 = (f32[128,256]{0,1:T(8,128)S(1)}, f32[128,256]{0,1:T(8,128)S(1)}, u32[]{:S(2)}, u32[]{:S(2)}) collective-permute-start(f32[128,256]{0,1:T(8,128)S(1)} %pad_maximum_fusion), channel_id=1, source_target_pairs={{0,2},{2,4},{4,6},{6,8},{8,10},{10,12},{12,14},{14,16},{16,18},{18... | collective-permute-start | bytes 393224 | tf_op jit(solution)/shard_map/ppermute | solution.py:133
  105.7 14.9 %collective-permute-start.18 = (f32[128,256]{0,1:T(8,128)S(1)}, f32[128,256]{0,1:T(8,128)S(1)}, u32[]{:S(2)}, u32[]{:S(2)}) collective-permute-start(f32[128,256]{0,1:T(8,128)S(1)} %pad_maximum_fusion.1), channel_id=1, source_target_pairs={{0,4},{2,6},{4,8},{6,10},{8,12},{10,14},{12,16},{14,18},{16,20},{1... | collective-permute-start | bytes 393224 | tf_op jit(solution)/shard_map/ppermute | solution.py:133
  107.7 16.7 %collective-permute-start.19 = (f32[128,256]{0,1:T(8,128)S(1)}, f32[128,256]{0,1:T(8,128)S(1)}, u32[]{:S(2)}, u32[]{:S(2)}) collective-permute-start(f32[128,256]{0,1:T(8,128)S(1)} %pad_maximum_fusion.2), channel_id=1, source_target_pairs={{0,6},{2,8},{4,10},{6,12},{8,14},{10,16},{12,18},{14,20},{16,22},{... | collective-permute-start | bytes 393224 | tf_op jit(solution)/shard_map/ppermute | solution.py:133
  110.2 14.8 %collective-permute-start.20 = (f32[128,256]{0,1:T(8,128)S(1)}, f32[128,256]{0,1:T(8,128)S(1)}, u32[]{:S(2)}, u32[]{:S(2)}) collective-permute-start(f32[128,256]{0,1:T(8,128)S(1)} %pad_maximum_fusion.3), channel_id=1, source_target_pairs={{0,8},{2,10},{4,12},{6,14},{8,16},{10,18},{12,20},{14,22},{16,24},... | collective-permute-start | bytes 393224 | tf_op jit(solution)/shard_map/ppermute | solution.py:133

commit v2 on v1

v2 whole, which is shorter than its diff:
```python
import jax
import jax.numpy as jnp
from jax import lax
from jax.experimental import pallas as pl
from jax.experimental.pallas import tpu as pltpu
from jax.sharding import PartitionSpec as P

NSUB = 128
ROW = 4
GROUP = 16
CHUNK = 2048
VMEM = 24 * 2**20


def shift(value, distance):
    route = [((s + distance) % NSUB, s) for s in range(NSUB)]
    return lax.ppermute(value, "sub", route)


def swap(value):
    return lax.ppermute(value, "col", [(0, 1), (1, 0)])


def weights_kernel(rows, cols, live, core, p0, p1, tiles, out, pt, acc, seen):
    o = pl.program_id(0)
    edge = tiles.shape[-1]
    nt = p0.shape[0] // edge

    @pl.when(o == 0)
    def _():
        for t in range(nt):
            seen[t] = 0
        seen[nt] = 0

    for at, half in enumerate((p0, p1)):

        @pl.when((o == 0) & (core[0] == 0))
        def _():
            for t in range(nt):
                pt[t, at * edge : (at + 1) * edge, :] = half[t * edge : (t + 1) * edge, :].T

        @pl.when((o == 0) & (core[0] == 1))
        def _():
            for t in range(nt):
                pt[t, (1 - at) * edge : (2 - at) * edge, :] = half[t * edge : (t + 1) * edge, :].T

    n = live[o]

    def group(g, carry):
        parts = []
        for j in range(GROUP):
            p = g * GROUP + j
            parts.append(
                jnp.dot(pt[rows[o, p]], tiles[0, p], preferred_element_type=jnp.float32)
            )
        for j in range(GROUP):
            p = g * GROUP + j
            c = jnp.where(p < n, cols[o, p], nt)
            fresh = seen[c] != o + 1
            seen[c] = o + 1
            acc[c] = jnp.where(fresh, parts[j], acc[c] + parts[j])
        return carry

    lax.fori_loop(0, (n + GROUP - 1) // GROUP, group, 0)
    for t in range(nt):
        out[0, :, t * edge : (t + 1) * edge] = jnp.where(seen[t] == o + 1, acc[t], 0.0).astype(
            out.dtype
        )


def weights(rows, cols, live, core, p0, p1, tiles):
    offsets, slots, edge, _ = tiles.shape
    fine = p0.shape[0]
    nt = fine // edge
    whole = lambda o, *_: (0, 0)
    return pl.pallas_call(
        weights_kernel,
        grid_spec=pltpu.PrefetchScalarGridSpec(
            num_scalar_prefetch=4,
            grid=(offsets,),
            in_specs=[
                pl.BlockSpec((fine, edge), whole),
                pl.BlockSpec((fine, edge), whole),
                pl.BlockSpec((1, slots, edge, edge), lambda o, *_: (o, 0, 0, 0)),
            ],
            out_specs=pl.BlockSpec((1, 2 * edge, fine), lambda o, *_: (o, 0, 0)),
            scratch_shapes=[
                pltpu.VMEM((nt, 2 * edge, edge), jnp.bfloat16),
                pltpu.VMEM((nt + 1, 2 * edge, edge), jnp.float32),
                pltpu.SMEM((nt + 1,), jnp.int32),
            ],
        ),
        out_shape=jax.ShapeDtypeStruct((offsets, 2 * edge, fine), jnp.bfloat16),
        compiler_params=pltpu.CompilerParams(vmem_limit_bytes=VMEM),
        cost_estimate=pl.CostEstimate(flops=1, bytes_accessed=1, transcendentals=0),
    )(rows, cols, live, core, p0, p1, tiles)


def tied(value, *others):
    return lax.optimization_barrier((value, *others))[0]


def blocks_kernel(plan, choice, core, mine, theirs, *rest):
    panels, (keep, give, acc) = rest[:-3], rest[-3:]
    j, k = pl.program_id(0), pl.program_id(1)
    width = keep.shape[-1]

    @pl.when(k == 0)
    def _():
        acc[...] = jnp.zeros_like(acc)

    for at, offset in enumerate(plan):
        for chunk, options in enumerate(offset):
            for pick, which in options:
                here = (j == at) & (k == chunk)

                @pl.when(here if pick is None else here & (choice[0] == pick))
                def _():
                    panel = panels[which][...]
                    acc[...] += jnp.dot(
                        mine[0], panel, preferred_element_type=jnp.float32
                    ) + jnp.dot(theirs[0], panel, preferred_element_type=jnp.float32)

    @pl.when(k == pl.num_programs(1) - 1)
    def _():
        keep[0] = acc[pl.ds(pl.multiple_of(core[0] * width, width), width), :]
        give[0] = acc[pl.ds(pl.multiple_of((1 - core[0]) * width, width), width), :]


def blocks(offsets, pieces, choice, core, mine, theirs):
    width = theirs.shape[1] // 2
    chunks = theirs.shape[2] // CHUNK
    arrays, specs, plan = [], [], []
    for o in offsets:
        plan.append([])
        for options in pieces[o]:
            plan[-1].append([])
            for pick, array, block in options:
                plan[-1][-1].append((pick, len(arrays)))
                arrays.append(array)
                specs.append(pl.BlockSpec((CHUNK, width), lambda j, k, *_, block=block: (block, 0)))

    def factor(j, k, *_):
        return (sum(jnp.where(j == at, o, 0) for at, o in enumerate(offsets)), 0, k)

    return pl.pallas_call(
        lambda *refs: blocks_kernel(plan, *refs),
        grid_spec=pltpu.PrefetchScalarGridSpec(
            num_scalar_prefetch=2,
            grid=(len(offsets), chunks),
            in_specs=[pl.BlockSpec((1, 2 * width, CHUNK), factor)] * 2 + specs,
            out_specs=[pl.BlockSpec((1, width, width), lambda j, k, *_: (j, 0, 0))] * 2,
            scratch_shapes=[pltpu.VMEM((2 * width, width), jnp.float32)],
        ),
        out_shape=[jax.ShapeDtypeStruct((len(offsets), width, width), jnp.float32)] * 2,
        compiler_params=pltpu.CompilerParams(vmem_limit_bytes=VMEM),
        cost_estimate=pl.CostEstimate(flops=1, bytes_accessed=1, transcendentals=0),
    )(choice, core, mine, theirs, *arrays)


def on_device(prolong, tiles, tile_rows, tile_cols, counts):
    slots = tiles.shape[2]
    offsets = tiles.shape[1]
    half = prolong.shape[0] // 2
    core = lax.axis_index("col")
    sub = lax.axis_index("sub")

    away = [(s, (s - 1) % NSUB) for s in range(NSUB) if s % ROW != 0]
    wrap = [(s, s + ROW - 1) for s in range(NSUB) if s % ROW == 0]
    y = shift(prolong, 4)
    near = lax.ppermute(prolong, "sub", away)

    other = swap(prolong)
    live = jnp.clip(counts[0] - core * slots, 0, slots)
    live = jnp.where(sub + jnp.arange(offsets) < NSUB, live, 0).astype(jnp.int32)
    which = jnp.reshape(core, (1,)).astype(jnp.int32)
    last = jnp.reshape(sub % ROW == ROW - 1, (1,)).astype(jnp.int32)
    mine = weights(tile_rows[0], tile_cols[0], live, which, prolong, other, tiles[0])
    theirs = swap(tied(mine, y))

    def found(wanted, pieces):
        return blocks(wanted, pieces, last, which, mine, theirs)

    def rows_of(keep, give):
        got = swap(give)
        return jnp.where(
            core == 0, jnp.concatenate([keep, got], axis=2), jnp.concatenate([got, keep], axis=2)
        )

    def moved(upper, o):
        return lax.ppermute(upper, "sub", [(s, s + o) for s in range(NSUB - o)])

    whole = lambda v: [[(None, v, 0)], [(None, v, 1)]]
    b = shift(y, -1)
    w = lax.ppermute(y, "sub", wrap)
    first = found((0, 4), {0: whole(prolong), 4: whole(y)})
    b_a, p_b = b[:half], near[half:] + w[half:]
    d_b = shift(p_b, 1)
    d_a = shift(b_a, -1)
    pieces = {3: whole(b), 1: [[(0, near, k), (1, w, k)] for k in range(2)]}
    second = found((1, 3), pieces)
    third = found((2,), {2: [[(None, d_a, 0)], [(None, d_b, 0)]]})
    keep, give = (jnp.concatenate(parts) for parts in zip(first, second, third))
    rows = rows_of(keep, give)
    order = (0, 4, 1, 3, 2)
    uppers = {o: rows[k] for k, o in enumerate(order)}
    lowers = {o: moved(uppers[o], o) for o in order[1:]}
    upper = jnp.stack([uppers[o] for o in range(offsets)])
    lower = jnp.stack([lowers[o].T for o in range(1, offsets)])
    return upper[None], lower[None]


def solution(mesh):
    placed = (
        P("sub", "col"),
        P("sub", None, "col", None, None),
        P("sub", None, "col"),
        P("sub", None, "col"),
        P("sub", None),
    )
    return jax.shard_map(
        on_device,
        mesh=mesh,
        in_specs=placed,
        out_specs=(P("sub", None, "col", None), P("sub", None, None, "col")),
        check_vma=False,
    )
```

time: 126 us -> 110 us (0.87); the launches traced: 126 us -> 109 us
  waiting for transfers between devices: 56.4 us -> 43 us
  matrix products: 9.87 us -> 0 us
  Pallas kernels: 18.9 us -> 23.7 us
  starting transfers between devices: 31.2 us -> 28 us
  local copies, waits for them, and re-layouts: 5.07 us -> 8.09 us
  other arithmetic: 3.31 us -> 4.95 us
    pallas_call x0 -> x2, Pallas kernels: none -> 11.4 us  [blocks(): pl.pallas_call(lambda *refs: blocks_kernel(plan, *refs), grid_spec=pltpu....]
    dot_general x20 -> x0, matrix products: 9.87 us -> none  [dot(): return jnp.dot(w, p, preferred_element_type=jnp.float32)]
    ppermute x8 -> x6, waiting for transfers between devices: 20.5 us -> 12.8 us  [the longest x4 12.8 us: moved(): return lax.ppermute(upper, 'sub', [(s, s + o) for s in range(NSUB - o)])]
    pallas_call x1, Pallas kernels: 18.9 us -> 12.2 us  [weights(): pl.pallas_call(weights_kernel, grid_spec=pltpu.PrefetchScalarGridSpec(num...]
    ppermute x6 -> x4, waiting for transfers between devices: 34.4 us -> 28.6 us  [shift(): return lax.ppermute(value, 'sub', route)]
    ppermute x8 -> x6, starting transfers between devices: 20.5 us -> 16.2 us  [the longest x4 8.98 us: moved(): return lax.ppermute(upper, 'sub', [(s, s + o) for s in range(NSUB - o)])]
    pallas_call x0 -> x1, other arithmetic: none -> 3.34 us  [blocks(): pl.pallas_call(lambda *refs: blocks_kernel(plan, *refs), grid_spec=pltpu....]
    ppermute x6 -> x4, starting transfers between devices: 8.88 us -> 11.6 us  [shift(): return lax.ppermute(value, 'sub', route)]
  transfers between devices with their start and end apart: 21 -> 13, of which waited for: 11 -> 7; matrix products, arithmetic and copies ran while one was open for 10% -> 3% of each run, Pallas kernels for 0% -> 22%
where the time goes in v2:
time: 110 us; the launch traced here: 109 us
  waiting for transfers between devices  43 us (39%)
  starting transfers between devices  28 us (25%)
  Pallas kernels  23.7 us (22%)
  local copies, waits for them, and re-layouts  8.09 us (7%)
  other arithmetic  4.95 us (4%)
    ppermute x4, waiting for transfers between devices, shift(): return lax.ppermute(value, 'sub', route)  28.6 us
    ppermute x4, waiting for transfers between devices, moved(): return lax.ppermute(upper, 'sub', [(s, s + o) for s in range(NSUB - o)])  12.8 us
    pallas_call x1, Pallas kernels, weights(): pl.pallas_call(weights_kernel, grid_spec=pltpu.PrefetchScalarGridSpec(num...  12.2 us
    ppermute x4, starting transfers between devices, shift(): return lax.ppermute(value, 'sub', route)  11.6 us
    pallas_call x2, Pallas kernels, blocks(): pl.pallas_call(lambda *refs: blocks_kernel(plan, *refs), grid_spec=pltpu....  11.4 us
    ppermute x4, starting transfers between devices, moved(): return lax.ppermute(upper, 'sub', [(s, s + o) for s in range(NSUB - o)])  8.98 us
    unnamed x20, local copies, waits for them, and re-layouts  7.22 us
    ppermute x1, starting transfers between devices, on_device(): w = lax.ppermute(y, 'sub', wrap)  5.94 us
  transfers between devices with their start and end apart: 13, of which 7 were waited for; matrix products, arithmetic and copies ran while one was open for 3% of the time, Pallas kernels for 22%

profile of v2, /device:TPU:128, one launch (start us, length us, event | category | flops | bytes accessed | tf_op | source)
XLA Modules:
  0.0 108.5 jit_solution(13787326999220664029)
XLA Ops:
  0.6 0.1 collective-permute-start
  0.7 2.6 %collective-permute-start.1 = (bf16[4096,128]{1,0:T(8,128)(2,1)}, bf16[4096,128]{1,0:T(8,128)(2,1)}, u32[]{:S(2)}, u32[]{:S(2)}) collective-permute-start(bf16[4096,128]{1,0:T(8,128)(2,1)} %refs_5_.1), channel_id=1, source_target_pairs={{8,0},{10,2},{12,4},{14,6},{16,8},{18,10},{20,12},{22,14},{24,16},... | collective-permute-start | bytes 3145736 | tf_op jit(solution)/shard_map/ppermute | solution.py:17
  3.4 0.7 compare_select_fusion.live
  4.0 0.7 copy_bitcast_fusion
  4.7 1.2 %copy-done = bf16[4096,128]{1,0:T(8,128)(2,1)S(1)} copy-done((bf16[4096,128]{1,0:T(8,128)(2,1)S(1)}, bf16[4096,128]{1,0:T(8,128)(2,1)}, u32[]{:S(2)}) %copy-start) | copy-done | bytes 1048600
  6.0 3.2 %copy-done.2 = bf16[1,5,48,128,128]{4,3,2,1,0:T(8,128)(2,1)S(1)} copy-done((bf16[1,5,48,128,128]{4,3,2,1,0:T(8,128)(2,1)S(1)}, bf16[1,5,48,128,128]{4,3,2,1,0:T(8,128)(2,1)}, u32[]{:S(2)}) %copy-start.2) | copy-done | bytes 7864344
  9.2 12.2 %shard_map.68.refs_2_ = bf16[5,256,4096]{2,1,0:T(8,128)(2,1)} custom-call(s32[5,48]{1,0:T(8,128)S(1)} %get-tuple-element.28.rows, s32[5,48]{1,0:T(8,128)S(1)} %get-tuple-element.27.cols, s32[5]{0:T(128)S(1)} %compare_select_fusion.live, s32[1]{0:T(128)} %bitcast.1.core.refs_1_, bf16[4096,128]{1,0:T(8,128)(2,1)S(1)} %copy-done, ...), custom_call_target="tpu_custom_call" | custom-call | flops 1 | bytes 1 | tf_op jit(solution)/shard_map/pallas_call | solution.py:76
  21.4 5.3 %collective-permute-done.1.refs_6_.refs_7_ = bf16[4096,128]{1,0:T(8,128)(2,1)} collective-permute-done((bf16[4096,128]{1,0:T(8,128)(2,1)}, bf16[4096,128]{1,0:T(8,128)(2,1)}, u32[]{:S(2)}, u32[]{:S(2)}) %collective-permute-start.1) | collective-permute-done | bytes 1048608 | tf_op jit(solution)/shard_map/ppermute | solution.py:17
  26.7 1.5 %collective-permute-start.5 = (bf16[4096,128]{1,0:T(8,128)(2,1)}, bf16[4096,128]{1,0:T(8,128)(2,1)S(1)}, u32[]{:S(2)}, u32[]{:S(2)}) collective-permute-start(bf16[4096,128]{1,0:T(8,128)(2,1)} %collective-permute-done.1.refs_6_.refs_7_), channel_id=1, source_target_pairs={{254,0},{0,2},{2,4},{4,6},{6,8},{8,10},{10,12},{12,14},{14,16},{16... | collective-permute-start | bytes 3145736 | tf_op jit(solution)/shard_map/ppermute | solution.py:17
  28.2 1.3 %collective-permute-start.3 = (bf16[4096,128]{1,0:T(8,128)(2,1)S(1)}, bf16[4096,128]{1,0:T(8,128)(2,1)S(1)}, u32[]{:S(2)}, u32[]{:S(2)}) collective-permute-start(bf16[4096,128]{1,0:T(8,128)(2,1)S(1)} %copy-done), channel_id=1, source_target_pairs={{2,0},{4,2},{6,4},{10,8},{12,10},{14,12},{18,16},{20,18},{22,20},{... | collective-permute-start | bytes 3145736 | tf_op jit(solution)/shard_map/ppermute | solution.py:171
  29.5 5.9 %collective-permute-start.4 = (bf16[4096,128]{1,0:T(8,128)(2,1)}, bf16[4096,128]{1,0:T(8,128)(2,1)S(1)}, u32[]{:S(2)}, u32[]{:S(2)}) collective-permute-start(bf16[4096,128]{1,0:T(8,128)(2,1)} %collective-permute-done.1.refs_6_.refs_7_), channel_id=1, source_target_pairs={{0,6},{8,14},{16,22},{24,30},{32,38},{40,46},{48,54},{56,62},{64,7... | collective-permute-start | bytes 3145736 | tf_op jit(solution)/shard_map/ppermute | solution.py:195
  35.4 23.3 %collective-permute-done.5.refs_8_.refs_9_ = bf16[4096,128]{1,0:T(8,128)(2,1)S(1)} collective-permute-done((bf16[4096,128]{1,0:T(8,128)(2,1)}, bf16[4096,128]{1,0:T(8,128)(2,1)S(1)}, u32[]{:S(2)}, u32[]{:S(2)}) %collective-permute-start.5) | collective-permute-done | bytes 1048608 | tf_op jit(solution)/shard_map/ppermute | solution.py:17
  58.7 0.8 slice.32
  59.6 0.0 collective-permute-start.6
  59.6 0.8 slice_add_fusion
  60.4 1.0 copy-done.3
  61.4 7.5 %collective-permute-start.7 = (bf16[2048,128]{1,0:T(8,128)(2,1)}, bf16[2048,128]{1,0:T(8,128)(2,1)}, u32[]{:S(2)}, u32[]{:S(2)}) collective-permute-start(bf16[2048,128]{1,0:T(8,128)(2,1)} %slice_add_fusion), channel_id=1, source_target_pairs={{2,0},{4,2},{6,4},{8,6},{10,8},{12,10},{14,12},{16,14},{18,16},{20... | collective-permute-start | bytes 1572872 | tf_op jit(solution)/shard_map/ppermute | solution.py:17
  68.9 5.9 %shard_map.69 = (f32[2,128,128]{2,1,0:T(8,128)S(1)}, f32[2,128,128]{2,1,0:T(8,128)S(1)}) custom-call(s32[1]{0:T(128)} %bitcast.refs_0_, s32[1]{0:T(128)} %bitcast.1.core.refs_1_, bf16[5,256,4096]{2,1,0:T(8,128)(2,1)} %shard_map.68.refs_2_, bf16[5,256,4096]{2,1,0:T(8,128)(2,1)} %collective-permute-done.2.refs_3_, bf16[4096,128]{1,0:T(8,128)(2,1)S(1)} %copy-done.1, ...), custom_call_target="tpu_custom_call" | custom-call | flops 1 | bytes 1 | tf_op jit(solution)/shard_map/pallas_call | solution.py:146
  74.8 5.5 %shard_map.70 = (f32[2,128,128]{2,1,0:T(8,128)S(1)}, f32[2,128,128]{2,1,0:T(8,128)S(1)}) custom-call(s32[1]{0:T(128)} %bitcast.refs_0_, s32[1]{0:T(128)} %bitcast.1.core.refs_1_, bf16[5,256,4096]{2,1,0:T(8,128)(2,1)} %shard_map.68.refs_2_, bf16[5,256,4096]{2,1,0:T(8,128)(2,1)} %collective-permute-done.2.refs_3_, ...), custom_call_target="tpu_custom_call" | custom-call | flops 1 | bytes 1 | tf_op jit(solution)/shard_map/pallas_call | solution.py:146
  80.4 3.3 %shard_map.71 = (f32[5,128,128]{2,1,0:T(8,128)S(1)}, f32[1,128,128]{2,1,0:T(8,128)S(1)}) fusion(f32[5,128,128]{2,1,0:T(8,128)S(1)} %constant_dynamic-update-slice_fusion.1, s32[1]{0:T(128)} %bitcast.refs_0_, s32[1]{0:T(128)} %bitcast.1.core.refs_1_, bf16[5,256,4096]{2,1,0:T(8,128)(2,1)} %shard_map.68.refs_2_, ...), kind=kCustom, calls=%fused_computation.13 | custom fusion | flops 1 | bytes 22151176 | tf_op jit(solution)/shard_map/pallas_call | solution.py:146
  83.8 0.1 collective-permute-start.8
  83.9 1.6 %collective-permute-done.8 = f32[5,128,128]{2,1,0:T(8,128)S(1)} collective-permute-done((f32[5,128,128]{2,1,0:T(8,128)S(1)}, f32[5,128,128]{2,1,0:T(8,128)S(1)}, u32[]{:S(2)}, u32[]{:S(2)}) %collective-permute-start.8) | collective-permute-done | bytes 327712 | tf_op jit(solution)/shard_map/ppermute | solution.py:21
  85.7 0.0 copy-start.5
  85.7 1.9 %collective-permute-start.12 = (f32[128,256]{1,0:T(8,128)S(1)}, f32[128,256]{1,0:T(8,128)S(1)}, u32[]{:S(2)}, u32[]{:S(2)}) collective-permute-start(f32[128,256]{1,0:T(8,128)S(1)} %get-tuple-element.25), channel_id=1, source_target_pairs={{0,8},{2,10},{4,12},{6,14},{8,16},{10,18},{12,20},{14,22},{16,24},... | collective-permute-start | bytes 393224 | tf_op jit(solution)/shard_map/ppermute | solution.py:191
  87.6 1.9 %collective-permute-start.11 = (f32[128,256]{1,0:T(8,128)S(1)}, f32[128,256]{1,0:T(8,128)S(1)}, u32[]{:S(2)}, u32[]{:S(2)}) collective-permute-start(f32[128,256]{1,0:T(8,128)S(1)} %get-tuple-element.24), channel_id=1, source_target_pairs={{0,6},{2,8},{4,10},{6,12},{8,14},{10,16},{12,18},{14,20},{16,22},{... | collective-permute-start | bytes 393224 | tf_op jit(solution)/shard_map/ppermute | solution.py:191
  89.6 1.9 %collective-permute-start.10 = (f32[128,256]{1,0:T(8,128)S(1)}, f32[128,256]{1,0:T(8,128)S(1)}, u32[]{:S(2)}, u32[]{:S(2)}) collective-permute-start(f32[128,256]{1,0:T(8,128)S(1)} %get-tuple-element.23), channel_id=1, source_target_pairs={{0,4},{2,6},{4,8},{6,10},{8,12},{10,14},{12,16},{14,18},{16,20},{1... | collective-permute-start | bytes 393224 | tf_op jit(solution)/shard_map/ppermute | solution.py:191
  91.5 3.2 %collective-permute-start.9 = (f32[128,256]{1,0:T(8,128)S(1)}, f32[128,256]{1,0:T(8,128)S(1)}, u32[]{:S(2)}, u32[]{:S(2)}) collective-permute-start(f32[128,256]{1,0:T(8,128)S(1)} %get-tuple-element.22), channel_id=1, source_target_pairs={{0,2},{2,4},{4,6},{6,8},{8,10},{10,12},{12,14},{14,16},{16,18},{18... | collective-permute-start | bytes 393224 | tf_op jit(solution)/shard_map/ppermute | solution.py:191
  94.7 1.7 %collective-permute-done.12 = f32[128,256]{1,0:T(8,128)S(1)} collective-permute-done((f32[128,256]{1,0:T(8,128)S(1)}, f32[128,256]{1,0:T(8,128)S(1)}, u32[]{:S(2)}, u32[]{:S(2)}) %collective-permute-start.12) | collective-permute-done | bytes 131104 | tf_op jit(solution)/shard_map/ppermute | solution.py:191
  96.4 2.9 %collective-permute-done.11 = f32[128,256]{1,0:T(8,128)S(1)} collective-permute-done((f32[128,256]{1,0:T(8,128)S(1)}, f32[128,256]{1,0:T(8,128)S(1)}, u32[]{:S(2)}, u32[]{:S(2)}) %collective-permute-start.11) | collective-permute-done | bytes 131104 | tf_op jit(solution)/shard_map/ppermute | solution.py:191
  99.4 3.4 %collective-permute-done.10 = f32[128,256]{1,0:T(8,128)S(1)} collective-permute-done((f32[128,256]{1,0:T(8,128)S(1)}, f32[128,256]{1,0:T(8,128)S(1)}, u32[]{:S(2)}, u32[]{:S(2)}) %collective-permute-start.10) | collective-permute-done | bytes 131104 | tf_op jit(solution)/shard_map/ppermute | solution.py:191
  102.8 4.7 %collective-permute-done.9 = f32[128,256]{1,0:T(8,128)S(1)} collective-permute-done((f32[128,256]{1,0:T(8,128)S(1)}, f32[128,256]{1,0:T(8,128)S(1)}, u32[]{:S(2)}, u32[]{:S(2)}) %collective-permute-start.9) | collective-permute-done | bytes 131104 | tf_op jit(solution)/shard_map/ppermute | solution.py:191
  107.5 1.0 copy.7
  (25 shorter events, 0.2 us)
Async XLA Ops:
  0.6 4.1 %collective-permute-start = (bf16[4096,128]{1,0:T(8,128)(2,1)}, bf16[4096,128]{1,0:T(8,128)(2,1)S(1)}, u32[]{:S(2)}, u32[]{:S(2)}) collective-permute-start(bf16[4096,128]{1,0:T(8,128)(2,1)} %refs_5_.1), channel_id=1, source_target_pairs={{0,1},{1,0},{2,3},{3,2},{4,5},{5,4},{6,7},{7,6},{8,9},{9,8},{10,11... | collective-permute-start | bytes 3145736 | tf_op jit(solution)/shard_map/ppermute | solution.py:21
  0.7 26.0 %collective-permute-start.1 = (bf16[4096,128]{1,0:T(8,128)(2,1)}, bf16[4096,128]{1,0:T(8,128)(2,1)}, u32[]{:S(2)}, u32[]{:S(2)}) collective-permute-start(bf16[4096,128]{1,0:T(8,128)(2,1)} %refs_5_.1), channel_id=1, source_target_pairs={{8,0},{10,2},{12,4},{14,6},{16,8},{18,10},{20,12},{22,14},{24,16},... | collective-permute-start | bytes 3145736 | tf_op jit(solution)/shard_map/ppermute | solution.py:17
  4.7 1.2 %copy-start = (bf16[4096,128]{1,0:T(8,128)(2,1)S(1)}, bf16[4096,128]{1,0:T(8,128)(2,1)}, u32[]{:S(2)}) copy-start(bf16[4096,128]{1,0:T(8,128)(2,1)} %refs_5_.1) | copy-start | bytes 3145732
  6.0 3.2 %copy-start.2 = (bf16[1,5,48,128,128]{4,3,2,1,0:T(8,128)(2,1)S(1)}, bf16[1,5,48,128,128]{4,3,2,1,0:T(8,128)(2,1)}, u32[]{:S(2)}) copy-start(bf16[1,5,48,128,128]{4,3,2,1,0:T(8,128)(2,1)} %param.6) | copy-start | bytes 23592964
  9.2 59.7 %copy-start.1 = (bf16[4096,128]{1,0:T(8,128)(2,1)S(1)}, bf16[4096,128]{1,0:T(8,128)(2,1)}, u32[]{:S(2)}) copy-start(bf16[4096,128]{1,0:T(8,128)(2,1)} %refs_5_.1) | copy-start | bytes 3145732
  26.7 42.2 %collective-permute-start.2 = (bf16[5,256,4096]{2,1,0:T(8,128)(2,1)}, bf16[5,256,4096]{2,1,0:T(8,128)(2,1)}, u32[]{:S(2)}, u32[]{:S(2)}) collective-permute-start(bf16[5,256,4096]{2,1,0:T(8,128)(2,1)} %shard_map.68.refs_2_), channel_id=1, source_target_pairs={{0,1},{1,0},{2,3},{3,2},{4,5},{5,4},{6,7},{7,6},{8,9},{9,8},{10,11... | collective-permute-start | bytes 31457288 | tf_op jit(solution)/shard_map/ppermute | solution.py:21
  26.7 32.0 %collective-permute-start.5 = (bf16[4096,128]{1,0:T(8,128)(2,1)}, bf16[4096,128]{1,0:T(8,128)(2,1)S(1)}, u32[]{:S(2)}, u32[]{:S(2)}) collective-permute-start(bf16[4096,128]{1,0:T(8,128)(2,1)} %collective-permute-done.1.refs_6_.refs_7_), channel_id=1, source_target_pairs={{254,0},{0,2},{2,4},{4,6},{6,8},{8,10},{10,12},{12,14},{14,16},{16... | collective-permute-start | bytes 3145736 | tf_op jit(solution)/shard_map/ppermute | solution.py:17
  28.2 31.4 %collective-permute-start.3 = (bf16[4096,128]{1,0:T(8,128)(2,1)S(1)}, bf16[4096,128]{1,0:T(8,128)(2,1)S(1)}, u32[]{:S(2)}, u32[]{:S(2)}) collective-permute-start(bf16[4096,128]{1,0:T(8,128)(2,1)S(1)} %copy-done), channel_id=1, source_target_pairs={{2,0},{4,2},{6,4},{10,8},{12,10},{14,12},{18,16},{20,18},{22,20},{... | collective-permute-start | bytes 3145736 | tf_op jit(solution)/shard_map/ppermute | solution.py:171
  29.5 30.1 %collective-permute-start.4 = (bf16[4096,128]{1,0:T(8,128)(2,1)}, bf16[4096,128]{1,0:T(8,128)(2,1)S(1)}, u32[]{:S(2)}, u32[]{:S(2)}) collective-permute-start(bf16[4096,128]{1,0:T(8,128)(2,1)} %collective-permute-done.1.refs_6_.refs_7_), channel_id=1, source_target_pairs={{0,6},{8,14},{16,22},{24,30},{32,38},{40,46},{48,54},{56,62},{64,7... | collective-permute-start | bytes 3145736 | tf_op jit(solution)/shard_map/ppermute | solution.py:195
  59.6 20.8 %collective-permute-start.6 = (bf16[2048,128]{1,0:T(8,128)(2,1)}, bf16[2048,128]{1,0:T(8,128)(2,1)}, u32[]{:S(2)}, u32[]{:S(2)}) collective-permute-start(bf16[2048,128]{1,0:T(8,128)(2,1)} %slice.32), channel_id=1, source_target_pairs={{254,0},{0,2},{2,4},{4,6},{6,8},{8,10},{10,12},{12,14},{14,16},{16... | collective-permute-start | bytes 1572872 | tf_op jit(solution)/shard_map/ppermute | solution.py:17
  60.4 1.0 copy-start.3
  61.4 19.0 %collective-permute-start.7 = (bf16[2048,128]{1,0:T(8,128)(2,1)}, bf16[2048,128]{1,0:T(8,128)(2,1)}, u32[]{:S(2)}, u32[]{:S(2)}) collective-permute-start(bf16[2048,128]{1,0:T(8,128)(2,1)} %slice_add_fusion), channel_id=1, source_target_pairs={{2,0},{4,2},{6,4},{8,6},{10,8},{12,10},{14,12},{16,14},{18,16},{20... | collective-permute-start | bytes 1572872 | tf_op jit(solution)/shard_map/ppermute | solution.py:17
  68.9 5.9 %copy-start.4 = (bf16[4096,128]{1,0:T(8,128)(2,1)S(1)}, bf16[4096,128]{1,0:T(8,128)(2,1)}, u32[]{:S(2)}) copy-start(bf16[4096,128]{1,0:T(8,128)(2,1)} %copy-done.3) | copy-start | bytes 3145732
  83.8 1.7 %collective-permute-start.8 = (f32[5,128,128]{2,1,0:T(8,128)S(1)}, f32[5,128,128]{2,1,0:T(8,128)S(1)}, u32[]{:S(2)}, u32[]{:S(2)}) collective-permute-start(f32[5,128,128]{2,1,0:T(8,128)S(1)} %pad_maximum_fusion), channel_id=1, source_target_pairs={{0,1},{1,0},{2,3},{3,2},{4,5},{5,4},{6,7},{7,6},{8,9},{9,8},{10,11... | collective-permute-start | bytes 983048 | tf_op jit(solution)/shard_map/ppermute | solution.py:21
  85.7 22.8 %copy-start.5 = (f32[5,128,256]{2,1,0:T(8,128)}, f32[5,128,256]{2,1,0:T(8,128)S(1)}, u32[]{:S(2)}) copy-start(f32[5,128,256]{2,1,0:T(8,128)S(1)} %get-tuple-element.26) | copy-start | bytes 1966084
  85.7 10.8 %collective-permute-start.12 = (f32[128,256]{1,0:T(8,128)S(1)}, f32[128,256]{1,0:T(8,128)S(1)}, u32[]{:S(2)}, u32[]{:S(2)}) collective-permute-start(f32[128,256]{1,0:T(8,128)S(1)} %get-tuple-element.25), channel_id=1, source_target_pairs={{0,8},{2,10},{4,12},{6,14},{8,16},{10,18},{12,20},{14,22},{16,24},... | collective-permute-start | bytes 393224 | tf_op jit(solution)/shard_map/ppermute | solution.py:191
  87.6 11.8 %collective-permute-start.11 = (f32[128,256]{1,0:T(8,128)S(1)}, f32[128,256]{1,0:T(8,128)S(1)}, u32[]{:S(2)}, u32[]{:S(2)}) collective-permute-start(f32[128,256]{1,0:T(8,128)S(1)} %get-tuple-element.24), channel_id=1, source_target_pairs={{0,6},{2,8},{4,10},{6,12},{8,14},{10,16},{12,18},{14,20},{16,22},{... | collective-permute-start | bytes 393224 | tf_op jit(solution)/shard_map/ppermute | solution.py:191
  89.6 13.2 %collective-permute-start.10 = (f32[128,256]{1,0:T(8,128)S(1)}, f32[128,256]{1,0:T(8,128)S(1)}, u32[]{:S(2)}, u32[]{:S(2)}) collective-permute-start(f32[128,256]{1,0:T(8,128)S(1)} %get-tuple-element.23), channel_id=1, source_target_pairs={{0,4},{2,6},{4,8},{6,10},{8,12},{10,14},{12,16},{14,18},{16,20},{1... | collective-permute-start | bytes 393224 | tf_op jit(solution)/shard_map/ppermute | solution.py:191
  91.5 16.0 %collective-permute-start.9 = (f32[128,256]{1,0:T(8,128)S(1)}, f32[128,256]{1,0:T(8,128)S(1)}, u32[]{:S(2)}, u32[]{:S(2)}) collective-permute-start(f32[128,256]{1,0:T(8,128)S(1)} %get-tuple-element.22), channel_id=1, source_target_pairs={{0,2},{2,4},{4,6},{6,8},{8,10},{10,12},{12,14},{14,16},{16,18},{18... | collective-permute-start | bytes 393224 | tf_op jit(solution)/shard_map/ppermute | solution.py:191

commit v3 on v2

--- a/solution.py
+++ b/solution.py
@@ -191,13 +191,16 @@
         return lax.ppermute(upper, "sub", [(s, s + o) for s in range(NSUB - o)])
 
     whole = lambda v: [[(None, v, 0)], [(None, v, 1)]]
-    b = shift(y, -1)
+    b_b = shift(prolong[half:], 3)
+    b_a = shift(y[:half], -1)
     w = lax.ppermute(y, "sub", wrap)
     first = found((0, 4), {0: whole(prolong), 4: whole(y)})
-    b_a, p_b = b[:half], near[half:] + w[half:]
-    d_b = shift(p_b, 1)
     d_a = shift(b_a, -1)
-    pieces = {3: whole(b), 1: [[(0, near, k), (1, w, k)] for k in range(2)]}
+    d_b = shift(near[half:] + w[half:], 1)
+    pieces = {
+        3: [[(None, b_a, 0)], [(None, b_b, 0)]],
+        1: [[(0, near, k), (1, w, k)] for k in range(2)],
+    }
     second = found((1, 3), pieces)
     third = found((2,), {2: [[(None, d_a, 0)], [(None, d_b, 0)]]})
     keep, give = (jnp.concatenate(parts) for parts in zip(first, second, third))

time: 110 us -> 109 us (level)
  waiting for transfers between devices: 43 us -> 37.8 us
  starting transfers between devices: 28 us -> 31.6 us
    ppermute x4 -> x5, waiting for transfers between devices: 28.6 us -> 23.5 us  [shift(): return lax.ppermute(value, 'sub', route)]
    ppermute x4 -> x5, starting transfers between devices: 11.6 us -> 15.1 us  [shift(): return lax.ppermute(value, 'sub', route)]
  transfers between devices with their start and end apart: 13 -> 14, of which waited for: 7 -> 7; matrix products, arithmetic and copies ran while one was open for 3% -> 3% of each run, Pallas kernels for 22% -> 22%
where the time goes in v3:
time: 109 us; the launch traced here: 107 us
  waiting for transfers between devices  37.8 us (35%)
  starting transfers between devices  31.6 us (29%)
  Pallas kernels  23.7 us (22%)
  local copies, waits for them, and re-layouts  8.15 us (7%)
  other arithmetic  4.95 us (5%)
    ppermute x5, waiting for transfers between devices, shift(): return lax.ppermute(value, 'sub', route)  23.5 us
    ppermute x5, starting transfers between devices, shift(): return lax.ppermute(value, 'sub', route)  15.1 us
    ppermute x4, waiting for transfers between devices, moved(): return lax.ppermute(upper, 'sub', [(s, s + o) for s in range(NSUB - o)])  12.6 us
    pallas_call x1, Pallas kernels, weights(): pl.pallas_call(weights_kernel, grid_spec=pltpu.PrefetchScalarGridSpec(num...  12.2 us
    pallas_call x2, Pallas kernels, blocks(): pl.pallas_call(lambda *refs: blocks_kernel(plan, *refs), grid_spec=pltpu....  11.5 us
    ppermute x4, starting transfers between devices, moved(): return lax.ppermute(upper, 'sub', [(s, s + o) for s in range(NSUB - o)])  8.84 us
    unnamed x20, local copies, waits for them, and re-layouts  7.24 us
    ppermute x1, starting transfers between devices, on_device(): w = lax.ppermute(y, 'sub', wrap)  6.24 us
  transfers between devices with their start and end apart: 14, of which 7 were waited for; matrix products, arithmetic and copies ran while one was open for 3% of the time, Pallas kernels for 22%

profile of v3, /device:TPU:128, one launch (start us, length us, event | category | flops | bytes accessed | tf_op | source)
XLA Modules:
  0.0 107.1 jit_solution(4765355069433514755)
XLA Ops:
  0.6 0.1 collective-permute-start
  0.7 2.6 %collective-permute-start.1 = (bf16[4096,128]{1,0:T(8,128)(2,1)}, bf16[4096,128]{1,0:T(8,128)(2,1)S(1)}, u32[]{:S(2)}, u32[]{:S(2)}) collective-permute-start(bf16[4096,128]{1,0:T(8,128)(2,1)} %refs_5_.1), channel_id=1, source_target_pairs={{8,0},{10,2},{12,4},{14,6},{16,8},{18,10},{20,12},{22,14},{24,16},... | collective-permute-start | bytes 3145736 | tf_op jit(solution)/shard_map/ppermute | solution.py:17
  3.4 0.7 compare_select_fusion.live
  4.0 0.7 copy_bitcast_fusion
  4.7 1.2 %copy-done = bf16[4096,128]{1,0:T(8,128)(2,1)S(1)} copy-done((bf16[4096,128]{1,0:T(8,128)(2,1)S(1)}, bf16[4096,128]{1,0:T(8,128)(2,1)}, u32[]{:S(2)}) %copy-start) | copy-done | bytes 1048600
  6.0 3.2 %copy-done.2 = bf16[1,5,48,128,128]{4,3,2,1,0:T(8,128)(2,1)S(1)} copy-done((bf16[1,5,48,128,128]{4,3,2,1,0:T(8,128)(2,1)S(1)}, bf16[1,5,48,128,128]{4,3,2,1,0:T(8,128)(2,1)}, u32[]{:S(2)}) %copy-start.2) | copy-done | bytes 7864344
  9.2 12.2 %shard_map.68.refs_2_ = bf16[5,256,4096]{2,1,0:T(8,128)(2,1)} custom-call(s32[5,48]{1,0:T(8,128)S(1)} %get-tuple-element.28.rows, s32[5,48]{1,0:T(8,128)S(1)} %get-tuple-element.27.cols, s32[5]{0:T(128)S(1)} %compare_select_fusion.live, s32[1]{0:T(128)} %bitcast.1.core.refs_1_, bf16[4096,128]{1,0:T(8,128)(2,1)S(1)} %copy-done, ...), custom_call_target="tpu_custom_call" | custom-call | flops 1 | bytes 1 | tf_op jit(solution)/shard_map/pallas_call | solution.py:76
  21.4 5.3 %collective-permute-done.1.refs_6_.refs_7_ = bf16[4096,128]{1,0:T(8,128)(2,1)S(1)} collective-permute-done((bf16[4096,128]{1,0:T(8,128)(2,1)}, bf16[4096,128]{1,0:T(8,128)(2,1)S(1)}, u32[]{:S(2)}, u32[]{:S(2)}) %collective-permute-start.1) | collective-permute-done | bytes 1048608 | tf_op jit(solution)/shard_map/ppermute | solution.py:17
  26.7 1.3 %collective-permute-start.3 = (bf16[4096,128]{1,0:T(8,128)(2,1)S(1)}, bf16[4096,128]{1,0:T(8,128)(2,1)S(1)}, u32[]{:S(2)}, u32[]{:S(2)}) collective-permute-start(bf16[4096,128]{1,0:T(8,128)(2,1)S(1)} %copy-done), channel_id=1, source_target_pairs={{2,0},{4,2},{6,4},{10,8},{12,10},{14,12},{18,16},{20,18},{22,20},{... | collective-permute-start | bytes 3145736 | tf_op jit(solution)/shard_map/ppermute | solution.py:171
  28.0 6.2 %collective-permute-start.4 = (bf16[4096,128]{1,0:T(8,128)(2,1)S(1)}, bf16[4096,128]{1,0:T(8,128)(2,1)S(1)}, u32[]{:S(2)}, u32[]{:S(2)}) collective-permute-start(bf16[4096,128]{1,0:T(8,128)(2,1)S(1)} %collective-permute-done.1.refs_6_.refs_7_), channel_id=1, source_target_pairs={{0,6},{8,14},{16,22},{24,30},{32,38},{40,46},{48,54},{56,62},{64,7... | collective-permute-start | bytes 3145736 | tf_op jit(solution)/shard_map/ppermute | solution.py:196
  34.3 0.1 collective-permute-start.5
  34.4 0.8 slice.28
  35.2 3.7 %collective-permute-start.6 = (bf16[2048,128]{1,0:T(8,128)(2,1)}, bf16[2048,128]{1,0:T(8,128)(2,1)}, u32[]{:S(2)}, u32[]{:S(2)}) collective-permute-start(bf16[2048,128]{1,0:T(8,128)(2,1)} %slice.28), channel_id=1, source_target_pairs={{6,0},{8,2},{10,4},{12,6},{14,8},{16,10},{18,12},{20,14},{22,16},{... | collective-permute-start | bytes 1572872 | tf_op jit(solution)/shard_map/ppermute | solution.py:17
  38.9 18.2 %collective-permute-done.5.refs_8_ = bf16[2048,128]{1,0:T(8,128)(2,1)} collective-permute-done((bf16[2048,128]{1,0:T(8,128)(2,1)S(1)}, bf16[2048,128]{1,0:T(8,128)(2,1)}, u32[]{:S(2)}, u32[]{:S(2)}) %collective-permute-start.5) | collective-permute-done | bytes 524320 | tf_op jit(solution)/shard_map/ppermute | solution.py:17
  57.2 2.6 %collective-permute-start.7 = (bf16[2048,128]{1,0:T(8,128)(2,1)}, bf16[2048,128]{1,0:T(8,128)(2,1)}, u32[]{:S(2)}, u32[]{:S(2)}) collective-permute-start(bf16[2048,128]{1,0:T(8,128)(2,1)} %collective-permute-done.5.refs_8_), channel_id=1, source_target_pairs={{254,0},{0,2},{2,4},{4,6},{6,8},{8,10},{10,12},{12,14},{14,16},{16... | collective-permute-start | bytes 1572872 | tf_op jit(solution)/shard_map/ppermute | solution.py:17
  59.8 0.8 slice_add_fusion
  60.6 1.0 copy-done.3
  61.6 6.0 %collective-permute-start.8 = (bf16[2048,128]{1,0:T(8,128)(2,1)}, bf16[2048,128]{1,0:T(8,128)(2,1)}, u32[]{:S(2)}, u32[]{:S(2)}) collective-permute-start(bf16[2048,128]{1,0:T(8,128)(2,1)} %slice_add_fusion), channel_id=1, source_target_pairs={{2,0},{4,2},{6,4},{8,6},{10,8},{12,10},{14,12},{16,14},{18,16},{20... | collective-permute-start | bytes 1572872 | tf_op jit(solution)/shard_map/ppermute | solution.py:17
  67.6 5.6 %shard_map.69 = (f32[2,128,128]{2,1,0:T(8,128)S(1)}, f32[2,128,128]{2,1,0:T(8,128)S(1)}) custom-call(s32[1]{0:T(128)} %bitcast.refs_0_, s32[1]{0:T(128)} %bitcast.1.core.refs_1_, bf16[5,256,4096]{2,1,0:T(8,128)(2,1)} %shard_map.68.refs_2_, bf16[5,256,4096]{2,1,0:T(8,128)(2,1)} %collective-permute-done.2.refs_3_, bf16[4096,128]{1,0:T(8,128)(2,1)S(1)} %copy-done.1, ...), custom_call_target="tpu_custom_call" | custom-call | flops 1 | bytes 1 | tf_op jit(solution)/shard_map/pallas_call | solution.py:146
  73.2 5.9 %shard_map.70 = (f32[2,128,128]{2,1,0:T(8,128)S(1)}, f32[2,128,128]{2,1,0:T(8,128)S(1)}) custom-call(s32[1]{0:T(128)} %bitcast.refs_0_, s32[1]{0:T(128)} %bitcast.1.core.refs_1_, bf16[5,256,4096]{2,1,0:T(8,128)(2,1)} %shard_map.68.refs_2_, bf16[5,256,4096]{2,1,0:T(8,128)(2,1)} %collective-permute-done.2.refs_3_, ...), custom_call_target="tpu_custom_call" | custom-call | flops 1 | bytes 1 | tf_op jit(solution)/shard_map/pallas_call | solution.py:146
  79.2 3.3 %shard_map.71 = (f32[5,128,128]{2,1,0:T(8,128)S(1)}, f32[1,128,128]{2,1,0:T(8,128)S(1)}) fusion(f32[5,128,128]{2,1,0:T(8,128)S(1)} %constant_dynamic-update-slice_fusion.1, s32[1]{0:T(128)} %bitcast.refs_0_, s32[1]{0:T(128)} %bitcast.1.core.refs_1_, bf16[5,256,4096]{2,1,0:T(8,128)(2,1)} %shard_map.68.refs_2_, ...), kind=kCustom, calls=%fused_computation.13 | custom fusion | flops 1 | bytes 22151176 | tf_op jit(solution)/shard_map/pallas_call | solution.py:146
  82.6 0.1 collective-permute-start.9
  82.7 1.6 %collective-permute-done.9 = f32[5,128,128]{2,1,0:T(8,128)S(1)} collective-permute-done((f32[5,128,128]{2,1,0:T(8,128)S(1)}, f32[5,128,128]{2,1,0:T(8,128)S(1)}, u32[]{:S(2)}, u32[]{:S(2)}) %collective-permute-start.9) | collective-permute-done | bytes 327712 | tf_op jit(solution)/shard_map/ppermute | solution.py:21
  84.5 1.9 %collective-permute-start.13 = (f32[128,256]{1,0:T(8,128)S(1)}, f32[128,256]{1,0:T(8,128)S(1)}, u32[]{:S(2)}, u32[]{:S(2)}) collective-permute-start(f32[128,256]{1,0:T(8,128)S(1)} %get-tuple-element.25), channel_id=1, source_target_pairs={{0,8},{2,10},{4,12},{6,14},{8,16},{10,18},{12,20},{14,22},{16,24},... | collective-permute-start | bytes 393224 | tf_op jit(solution)/shard_map/ppermute | solution.py:191
  86.4 2.2 %collective-permute-start.12 = (f32[128,256]{1,0:T(8,128)S(1)}, f32[128,256]{1,0:T(8,128)S(1)}, u32[]{:S(2)}, u32[]{:S(2)}) collective-permute-start(f32[128,256]{1,0:T(8,128)S(1)} %get-tuple-element.24), channel_id=1, source_target_pairs={{0,6},{2,8},{4,10},{6,12},{8,14},{10,16},{12,18},{14,20},{16,22},{... | collective-permute-start | bytes 393224 | tf_op jit(solution)/shard_map/ppermute | solution.py:191
  88.7 1.9 %collective-permute-start.11 = (f32[128,256]{1,0:T(8,128)S(1)}, f32[128,256]{1,0:T(8,128)S(1)}, u32[]{:S(2)}, u32[]{:S(2)}) collective-permute-start(f32[128,256]{1,0:T(8,128)S(1)} %get-tuple-element.23), channel_id=1, source_target_pairs={{0,4},{2,6},{4,8},{6,10},{8,12},{10,14},{12,16},{14,18},{16,20},{1... | collective-permute-start | bytes 393224 | tf_op jit(solution)/shard_map/ppermute | solution.py:191
  90.6 2.8 %collective-permute-start.10 = (f32[128,256]{1,0:T(8,128)S(1)}, f32[128,256]{1,0:T(8,128)S(1)}, u32[]{:S(2)}, u32[]{:S(2)}) collective-permute-start(f32[128,256]{1,0:T(8,128)S(1)} %get-tuple-element.22), channel_id=1, source_target_pairs={{0,2},{2,4},{4,6},{6,8},{8,10},{10,12},{12,14},{14,16},{16,18},{18... | collective-permute-start | bytes 393224 | tf_op jit(solution)/shard_map/ppermute | solution.py:191
  93.4 1.9 %collective-permute-done.13 = f32[128,256]{1,0:T(8,128)S(1)} collective-permute-done((f32[128,256]{1,0:T(8,128)S(1)}, f32[128,256]{1,0:T(8,128)S(1)}, u32[]{:S(2)}, u32[]{:S(2)}) %collective-permute-start.13) | collective-permute-done | bytes 131104 | tf_op jit(solution)/shard_map/ppermute | solution.py:191
  95.2 2.9 %collective-permute-done.12 = f32[128,256]{1,0:T(8,128)S(1)} collective-permute-done((f32[128,256]{1,0:T(8,128)S(1)}, f32[128,256]{1,0:T(8,128)S(1)}, u32[]{:S(2)}, u32[]{:S(2)}) %collective-permute-start.12) | collective-permute-done | bytes 131104 | tf_op jit(solution)/shard_map/ppermute | solution.py:191
  98.2 3.4 %collective-permute-done.11 = f32[128,256]{1,0:T(8,128)S(1)} collective-permute-done((f32[128,256]{1,0:T(8,128)S(1)}, f32[128,256]{1,0:T(8,128)S(1)}, u32[]{:S(2)}, u32[]{:S(2)}) %collective-permute-start.11) | collective-permute-done | bytes 131104 | tf_op jit(solution)/shard_map/ppermute | solution.py:191
  101.6 4.4 %collective-permute-done.10 = f32[128,256]{1,0:T(8,128)S(1)} collective-permute-done((f32[128,256]{1,0:T(8,128)S(1)}, f32[128,256]{1,0:T(8,128)S(1)}, u32[]{:S(2)}, u32[]{:S(2)}) %collective-permute-start.10) | collective-permute-done | bytes 131104 | tf_op jit(solution)/shard_map/ppermute | solution.py:191
  106.1 1.0 copy.7
  (28 shorter events, 0.3 us)
Async XLA Ops:
  0.6 4.1 %collective-permute-start = (bf16[4096,128]{1,0:T(8,128)(2,1)}, bf16[4096,128]{1,0:T(8,128)(2,1)S(1)}, u32[]{:S(2)}, u32[]{:S(2)}) collective-permute-start(bf16[4096,128]{1,0:T(8,128)(2,1)} %refs_5_.1), channel_id=1, source_target_pairs={{0,1},{1,0},{2,3},{3,2},{4,5},{5,4},{6,7},{7,6},{8,9},{9,8},{10,11... | collective-permute-start | bytes 3145736 | tf_op jit(solution)/shard_map/ppermute | solution.py:21
  0.7 26.0 %collective-permute-start.1 = (bf16[4096,128]{1,0:T(8,128)(2,1)}, bf16[4096,128]{1,0:T(8,128)(2,1)S(1)}, u32[]{:S(2)}, u32[]{:S(2)}) collective-permute-start(bf16[4096,128]{1,0:T(8,128)(2,1)} %refs_5_.1), channel_id=1, source_target_pairs={{8,0},{10,2},{12,4},{14,6},{16,8},{18,10},{20,12},{22,14},{24,16},... | collective-permute-start | bytes 3145736 | tf_op jit(solution)/shard_map/ppermute | solution.py:17
  4.7 1.2 %copy-start = (bf16[4096,128]{1,0:T(8,128)(2,1)S(1)}, bf16[4096,128]{1,0:T(8,128)(2,1)}, u32[]{:S(2)}) copy-start(bf16[4096,128]{1,0:T(8,128)(2,1)} %refs_5_.1) | copy-start | bytes 3145732
  6.0 3.2 %copy-start.2 = (bf16[1,5,48,128,128]{4,3,2,1,0:T(8,128)(2,1)S(1)}, bf16[1,5,48,128,128]{4,3,2,1,0:T(8,128)(2,1)}, u32[]{:S(2)}) copy-start(bf16[1,5,48,128,128]{4,3,2,1,0:T(8,128)(2,1)} %param.6) | copy-start | bytes 23592964
  9.2 58.5 %copy-start.1 = (bf16[4096,128]{1,0:T(8,128)(2,1)S(1)}, bf16[4096,128]{1,0:T(8,128)(2,1)}, u32[]{:S(2)}) copy-start(bf16[4096,128]{1,0:T(8,128)(2,1)} %refs_5_.1) | copy-start | bytes 3145732
  26.7 40.9 %collective-permute-start.2 = (bf16[5,256,4096]{2,1,0:T(8,128)(2,1)}, bf16[5,256,4096]{2,1,0:T(8,128)(2,1)}, u32[]{:S(2)}, u32[]{:S(2)}) collective-permute-start(bf16[5,256,4096]{2,1,0:T(8,128)(2,1)} %shard_map.68.refs_2_), channel_id=1, source_target_pairs={{0,1},{1,0},{2,3},{3,2},{4,5},{5,4},{6,7},{7,6},{8,9},{9,8},{10,11... | collective-permute-start | bytes 31457288 | tf_op jit(solution)/shard_map/ppermute | solution.py:21
  26.7 33.1 %collective-permute-start.3 = (bf16[4096,128]{1,0:T(8,128)(2,1)S(1)}, bf16[4096,128]{1,0:T(8,128)(2,1)S(1)}, u32[]{:S(2)}, u32[]{:S(2)}) collective-permute-start(bf16[4096,128]{1,0:T(8,128)(2,1)S(1)} %copy-done), channel_id=1, source_target_pairs={{2,0},{4,2},{6,4},{10,8},{12,10},{14,12},{18,16},{20,18},{22,20},{... | collective-permute-start | bytes 3145736 | tf_op jit(solution)/shard_map/ppermute | solution.py:171
  28.0 31.8 %collective-permute-start.4 = (bf16[4096,128]{1,0:T(8,128)(2,1)S(1)}, bf16[4096,128]{1,0:T(8,128)(2,1)S(1)}, u32[]{:S(2)}, u32[]{:S(2)}) collective-permute-start(bf16[4096,128]{1,0:T(8,128)(2,1)S(1)} %collective-permute-done.1.refs_6_.refs_7_), channel_id=1, source_target_pairs={{0,6},{8,14},{16,22},{24,30},{32,38},{40,46},{48,54},{56,62},{64,7... | collective-permute-start | bytes 3145736 | tf_op jit(solution)/shard_map/ppermute | solution.py:196
  34.3 22.9 %collective-permute-start.5 = (bf16[2048,128]{1,0:T(8,128)(2,1)S(1)}, bf16[2048,128]{1,0:T(8,128)(2,1)}, u32[]{:S(2)}, u32[]{:S(2)}) collective-permute-start(bf16[2048,128]{1,0:T(8,128)(2,1)S(1)} %slice.36), channel_id=1, source_target_pairs={{254,0},{0,2},{2,4},{4,6},{6,8},{8,10},{10,12},{12,14},{14,16},{16... | collective-permute-start | bytes 1572872 | tf_op jit(solution)/shard_map/ppermute | solution.py:17
  35.2 38.0 %collective-permute-start.6 = (bf16[2048,128]{1,0:T(8,128)(2,1)}, bf16[2048,128]{1,0:T(8,128)(2,1)}, u32[]{:S(2)}, u32[]{:S(2)}) collective-permute-start(bf16[2048,128]{1,0:T(8,128)(2,1)} %slice.28), channel_id=1, source_target_pairs={{6,0},{8,2},{10,4},{12,6},{14,8},{16,10},{18,12},{20,14},{22,16},{... | collective-permute-start | bytes 1572872 | tf_op jit(solution)/shard_map/ppermute | solution.py:17
  57.2 22.0 %collective-permute-start.7 = (bf16[2048,128]{1,0:T(8,128)(2,1)}, bf16[2048,128]{1,0:T(8,128)(2,1)}, u32[]{:S(2)}, u32[]{:S(2)}) collective-permute-start(bf16[2048,128]{1,0:T(8,128)(2,1)} %collective-permute-done.5.refs_8_), channel_id=1, source_target_pairs={{254,0},{0,2},{2,4},{4,6},{6,8},{8,10},{10,12},{12,14},{14,16},{16... | collective-permute-start | bytes 1572872 | tf_op jit(solution)/shard_map/ppermute | solution.py:17
  60.6 1.0 copy-start.3
  61.6 17.6 %collective-permute-start.8 = (bf16[2048,128]{1,0:T(8,128)(2,1)}, bf16[2048,128]{1,0:T(8,128)(2,1)}, u32[]{:S(2)}, u32[]{:S(2)}) collective-permute-start(bf16[2048,128]{1,0:T(8,128)(2,1)} %slice_add_fusion), channel_id=1, source_target_pairs={{2,0},{4,2},{6,4},{8,6},{10,8},{12,10},{14,12},{16,14},{18,16},{20... | collective-permute-start | bytes 1572872 | tf_op jit(solution)/shard_map/ppermute | solution.py:17
  67.6 5.6 %copy-start.4 = (bf16[4096,128]{1,0:T(8,128)(2,1)S(1)}, bf16[4096,128]{1,0:T(8,128)(2,1)}, u32[]{:S(2)}) copy-start(bf16[4096,128]{1,0:T(8,128)(2,1)} %copy-done.3) | copy-start | bytes 3145732
  82.6 1.7 %collective-permute-start.9 = (f32[5,128,128]{2,1,0:T(8,128)S(1)}, f32[5,128,128]{2,1,0:T(8,128)S(1)}, u32[]{:S(2)}, u32[]{:S(2)}) collective-permute-start(f32[5,128,128]{2,1,0:T(8,128)S(1)} %pad_maximum_fusion), channel_id=1, source_target_pairs={{0,1},{1,0},{2,3},{3,2},{4,5},{5,4},{6,7},{7,6},{8,9},{9,8},{10,11... | collective-permute-start | bytes 983048 | tf_op jit(solution)/shard_map/ppermute | solution.py:21
  84.5 22.6 %copy-start.5 = (f32[5,128,256]{2,1,0:T(8,128)}, f32[5,128,256]{2,1,0:T(8,128)S(1)}, u32[]{:S(2)}) copy-start(f32[5,128,256]{2,1,0:T(8,128)S(1)} %get-tuple-element.26) | copy-start | bytes 1966084
  84.5 10.8 %collective-permute-start.13 = (f32[128,256]{1,0:T(8,128)S(1)}, f32[128,256]{1,0:T(8,128)S(1)}, u32[]{:S(2)}, u32[]{:S(2)}) collective-permute-start(f32[128,256]{1,0:T(8,128)S(1)} %get-tuple-element.25), channel_id=1, source_target_pairs={{0,8},{2,10},{4,12},{6,14},{8,16},{10,18},{12,20},{14,22},{16,24},... | collective-permute-start | bytes 393224 | tf_op jit(solution)/shard_map/ppermute | solution.py:191
  86.4 11.7 %collective-permute-start.12 = (f32[128,256]{1,0:T(8,128)S(1)}, f32[128,256]{1,0:T(8,128)S(1)}, u32[]{:S(2)}, u32[]{:S(2)}) collective-permute-start(f32[128,256]{1,0:T(8,128)S(1)} %get-tuple-element.24), channel_id=1, source_target_pairs={{0,6},{2,8},{4,10},{6,12},{8,14},{10,16},{12,18},{14,20},{16,22},{... | collective-permute-start | bytes 393224 | tf_op jit(solution)/shard_map/ppermute | solution.py:191
  88.7 12.9 %collective-permute-start.11 = (f32[128,256]{1,0:T(8,128)S(1)}, f32[128,256]{1,0:T(8,128)S(1)}, u32[]{:S(2)}, u32[]{:S(2)}) collective-permute-start(f32[128,256]{1,0:T(8,128)S(1)} %get-tuple-element.23), channel_id=1, source_target_pairs={{0,4},{2,6},{4,8},{6,10},{8,12},{10,14},{12,16},{14,18},{16,20},{1... | collective-permute-start | bytes 393224 | tf_op jit(solution)/shard_map/ppermute | solution.py:191
  90.6 15.4 %collective-permute-start.10 = (f32[128,256]{1,0:T(8,128)S(1)}, f32[128,256]{1,0:T(8,128)S(1)}, u32[]{:S(2)}, u32[]{:S(2)}) collective-permute-start(f32[128,256]{1,0:T(8,128)S(1)} %get-tuple-element.22), channel_id=1, source_target_pairs={{0,2},{2,4},{4,6},{6,8},{8,10},{10,12},{12,14},{14,16},{16,18},{18... | collective-permute-start | bytes 393224 | tf_op jit(solution)/shard_map/ppermute | solution.py:191
